TPU v7x, 256 devices: a whole 4x4x8 slice. The times are simulated.
256 devices in a mesh: cuts: 8 (over y, core), rows: 32 (over x, z).
Axes of the slice: x: 4, y: 4, z: 8, core: 2. Of those that a mesh axis runs over, the one named last changes fastest.
Arguments:
- vectors: bfloat16 [65536, 1024], P('rows', 'cuts'), may hold values from -11.2 to 11.2
- blocks: bfloat16 [512, 8, 128, 128], P('rows'), may hold values from -0.1875 to 0.1875
- block_cols: int32 [512, 8], P('rows'), may hold values from 0 to 511, as said below
- counts: int32 [512], P('rows'), may hold values from 1 to 8, as said below
- lower_end: float32 [8], P('cuts'), may hold values from -2.4 to -1.9
- upper_end: float32 [8], P('cuts'), may hold values from 1.9 to 2.4
- coeffs: float32 [8, 7], P('cuts'), may hold values from -0.9 to 0.9
Outputs:
- projected: bfloat16 [65536, 1024], P('rows', 'cuts')
Inputs may be any that keep to these rules, and one draw needn't show every extreme that they name: `block_cols`: slot 0 names the row block itself; the first counts of a row block's slots name distinct row blocks at most 4 away from it; later slots name the row block itself. The first row block of every group of 16 names the row block 4 below it, and the last the row block 4 above it, where those exist. `counts`: row blocks of some devices hold far more live slots than others; 8 is reached.
All inputs are finite; a program needn't handle non-finite values.
Results may differ from a plain program's by a relative error of at most 0.0065.
Values may be sent and summed in bfloat16 or wider, within the bound.
A program may use at most 64 MiB of HBM per device.

v0:
```python
import jax
import jax.numpy as jnp
from jax import lax
from jax.sharding import PartitionSpec as P

NB = 32
W = 4
DEG = 6
PASSES = 2


def with_halo(block, sides, width):
    for axis, dim in sides:
        count = lax.axis_size(axis)
        forward = [(i, i + 1) for i in range(count - 1)]
        backward = [(target, source) for source, target in forward]
        low = lax.ppermute(
            lax.slice_in_dim(block, block.shape[dim] - width, None, axis=dim), axis, forward
        )
        high = lax.ppermute(lax.slice_in_dim(block, 0, width, axis=dim), axis, backward)
        block = jnp.concatenate([low, block, high], axis=dim)
    return block


def passed_along(value, axis, steps):
    count = lax.axis_size(axis)
    leading, last = (max(0, -steps), min(count, count - steps))
    return lax.ppermute(value, axis, [(source, source + steps) for source in range(leading, last)])


def gather_product(source, index, active, blocks):
    row_blocks, slot_count, block_size, _ = blocks.shape
    vec_cols = source.shape[2]
    spare_row = source.shape[0]
    padded_source = jnp.concatenate(
        [source, jnp.zeros((1, block_size, vec_cols), source.dtype)], axis=0
    )
    picked = jnp.where(active, index, spare_row)
    return jnp.einsum(
        "rsij,rsjv->riv", blocks, padded_source[picked], preferred_element_type=jnp.float32
    )


def apply_matrix(blocks, block_cols, counts, rounded, first_block):
    row_blocks, slot_count, block_size, _ = blocks.shape
    vec_cols = rounded.shape[1]
    slot_ids = jnp.arange(slot_count, dtype=jnp.int32)
    in_use = slot_ids[None, :] < counts[:, None]
    widened = with_halo(rounded, (("rows", 0),), W * block_size)
    widened = widened.reshape(row_blocks + 2 * W, block_size, vec_cols)
    summed = gather_product(widened, block_cols - first_block + W, in_use, blocks)
    return summed.reshape(row_blocks * block_size, vec_cols)


def body(vectors, blocks, block_cols, counts, lower_end, upper_end, coeffs):
    row_blocks = blocks.shape[0]
    vec_cols = vectors.shape[1]
    first_block = lax.axis_index("rows") * row_blocks
    centre = (lower_end + upper_end) * 0.5
    half_width = (upper_end - lower_end) * 0.5
    weights = coeffs[0]
    filtered = vectors.astype(jnp.float32)
    for pass_id in range(PASSES):
        previous = filtered
        summed = weights[0] * previous
        product = apply_matrix(
            blocks, block_cols, counts, previous.astype(jnp.bfloat16), first_block
        )
        current = (product - centre * previous) / half_width
        summed = summed + weights[1] * current
        for term_k in range(2, DEG + 1):
            product = apply_matrix(
                blocks, block_cols, counts, current.astype(jnp.bfloat16), first_block
            )
            upcoming = 2.0 * (product - centre * current) / half_width - previous
            previous, current = (current, upcoming)
            summed = summed + weights[term_k] * current
        filtered = summed
    filtered_low = filtered.astype(jnp.bfloat16)
    edge_vecs = filtered_low[:, vec_cols - NB :].T
    received = passed_along(edge_vecs, "cuts", 1)
    gram_part = jnp.dot(received, received.T, preferred_element_type=jnp.float32)
    cross_part = jnp.dot(received, filtered_low, preferred_element_type=jnp.float32)
    gram_sum, cross_sum = lax.psum((gram_part, cross_part), "rows")
    gram_sum = gram_sum + jnp.eye(NB, dtype=jnp.float32)
    factor = jnp.linalg.cholesky(gram_sum)
    solved = jax.scipy.linalg.cho_solve((factor, True), cross_sum).astype(jnp.bfloat16)
    correction = lax.dot_general(
        received, solved, (((0,), (0,)), ((), ())), preferred_element_type=jnp.float32
    )
    return (filtered - correction).astype(jnp.bfloat16)


def solution(mesh):
    return jax.shard_map(
        body,
        mesh=mesh,
        in_specs=(
            P("rows", "cuts"),
            P("rows", None, None, None),
            P("rows", None),
            P("rows"),
            P("cuts"),
            P("cuts"),
            P("cuts", None),
        ),
        out_specs=P("rows", "cuts"),
        check_vma=False,
    )
```

profile of v0, /device:TPU:8, one launch (start us, length us, event | category | flops | bytes accessed | tf_op | source)
XLA Modules:
  0.0 406.3 jit_solution(2596024404660017335)
XLA Ops:
  16.1 4.7 %fusion.79 = f32[16,128,128,1]{1,2,3,0:T(8,128)S(1)} fusion(bf16[16,8,128,128]{3,2,1,0:T(8,128)(2,1)} %param.8, bf16[16,8,128,128]{3,2,1,0:T(8,128)(2,1)} %bitcast.285), kind=kOutput, calls=%fused_computation.125 | convolution fusion | flops 536870912 | bytes 9437184 | tf_op jit(solution)/shard_map/rsij,rsjv->riv/dot_general | solution.py:39
  27.4 5.5 %collective-permute-done.3 = bf16[512,128]{1,0:T(8,128)(2,1)S(1)} collective-permute-done((bf16[512,128]{1,0:T(8,128)(2,1)S(1)}, bf16[512,128]{1,0:T(8,128)(2,1)S(1)}, u32[]{:S(2)}, u32[]{:S(2)}) %collective-permute-start.3) | collective-permute-done | bytes 131104 | tf_op jit(solution)/shard_map/ppermute | solution.py:20
  36.1 4.7 %fusion.80 = f32[16,128,128,1]{1,2,3,0:T(8,128)S(1)} fusion(bf16[16,8,128,128]{3,2,1,0:T(8,128)(2,1)} %param.8, bf16[16,8,128,128]{3,2,1,0:T(8,128)(2,1)} %bitcast.286), kind=kOutput, calls=%fused_computation.126 | convolution fusion | flops 536870912 | bytes 9437184 | tf_op jit(solution)/shard_map/rsij,rsjv->riv/dot_general | solution.py:39
  41.2 4.9 %collective-permute-start.4 = (bf16[512,128]{1,0:T(8,128)(2,1)S(1)}, bf16[512,128]{1,0:T(8,128)(2,1)S(1)}, u32[]{:S(2)}, u32[]{:S(2)}) collective-permute-start(bf16[512,128]{1,0:T(8,128)(2,1)S(1)} %get-tuple-element.37), channel_id=1, source_target_pairs={{0,1},{1,2},{2,3},{3,4},{4,5},{5,6},{6,7},{7,8},{8,9},{9,10},{10,1... | collective-permute-start | bytes 393224 | tf_op jit(solution)/shard_map/ppermute | solution.py:17
  56.2 4.7 %fusion.81 = f32[16,128,128,1]{1,2,3,0:T(8,128)S(1)} fusion(bf16[16,8,128,128]{3,2,1,0:T(8,128)(2,1)} %param.8, bf16[16,8,128,128]{3,2,1,0:T(8,128)(2,1)} %bitcast.287), kind=kOutput, calls=%fused_computation.127 | convolution fusion | flops 536870912 | bytes 9437184 | tf_op jit(solution)/shard_map/rsij,rsjv->riv/dot_general | solution.py:39
  68.7 4.4 %collective-permute-done.7 = bf16[512,128]{1,0:T(8,128)(2,1)S(1)} collective-permute-done((bf16[512,128]{1,0:T(8,128)(2,1)S(1)}, bf16[512,128]{1,0:T(8,128)(2,1)S(1)}, u32[]{:S(2)}, u32[]{:S(2)}) %collective-permute-start.7) | collective-permute-done | bytes 131104 | tf_op jit(solution)/shard_map/ppermute | solution.py:20
  76.3 4.8 %fusion.82 = f32[16,128,128,1]{1,2,3,0:T(8,128)S(1)} fusion(bf16[16,8,128,128]{3,2,1,0:T(8,128)(2,1)} %param.8, bf16[16,8,128,128]{3,2,1,0:T(8,128)(2,1)} %bitcast.288), kind=kOutput, calls=%fused_computation.128 | convolution fusion | flops 536870912 | bytes 9437184 | tf_op jit(solution)/shard_map/rsij,rsjv->riv/dot_general | solution.py:39
  87.0 4.4 %collective-permute-done.9 = bf16[512,128]{1,0:T(8,128)(2,1)S(1)} collective-permute-done((bf16[512,128]{1,0:T(8,128)(2,1)S(1)}, bf16[512,128]{1,0:T(8,128)(2,1)S(1)}, u32[]{:S(2)}, u32[]{:S(2)}) %collective-permute-start.9) | collective-permute-done | bytes 131104 | tf_op jit(solution)/shard_map/ppermute | solution.py:20
  94.6 4.8 %fusion.83 = f32[16,128,128,1]{1,2,3,0:T(8,128)S(1)} fusion(bf16[16,8,128,128]{3,2,1,0:T(8,128)(2,1)} %param.8, bf16[16,8,128,128]{3,2,1,0:T(8,128)(2,1)} %bitcast.289), kind=kOutput, calls=%fused_computation.129 | convolution fusion | flops 536870912 | bytes 9437184 | tf_op jit(solution)/shard_map/rsij,rsjv->riv/dot_general | solution.py:39
  113.2 4.8 %fusion.84 = f32[16,128,128,1]{1,2,3,0:T(8,128)S(1)} fusion(bf16[16,8,128,128]{3,2,1,0:T(8,128)(2,1)} %param.8, bf16[16,8,128,128]{3,2,1,0:T(8,128)(2,1)} %bitcast.290), kind=kOutput, calls=%fused_computation.130 | convolution fusion | flops 536870912 | bytes 9437184 | tf_op jit(solution)/shard_map/rsij,rsjv->riv/dot_general | solution.py:39
  118.0 6.7 %fusion.59 = (bf16[2048,128]{1,0:T(8,128)(2,1)S(1)}, f32[2048,128]{1,0:T(8,128)}) fusion(f32[16,128,128,1]{1,2,3,0:T(8,128)S(1)} %fusion.84, f32[]{:T(128)} %bitcast.38, f32[2048,128]{1,0:T(8,128)S(1)} %copy-done.15, f32[16,128,128,1]{1,2,3,0:T(8,128)S(1)} %copy-done.20, f32[]{:T(128)} %bitcast.31, f32[2048,128]{1,0:T(8,128)S(1)} %get-tuple-element.18, ...), kind=kLoop, calls=%fused_computation.107 | loop fusion | flops 8650752 | bytes 8388644 | tf_op jit(solution)/shard_map/convert_element_type | solution.py:67
  130.4 4.4 %collective-permute-done.13 = bf16[512,128]{1,0:T(8,128)(2,1)S(1)} collective-permute-done((bf16[512,128]{1,0:T(8,128)(2,1)S(1)}, bf16[512,128]{1,0:T(8,128)(2,1)S(1)}, u32[]{:S(2)}, u32[]{:S(2)}) %collective-permute-start.13) | collective-permute-done | bytes 131104 | tf_op jit(solution)/shard_map/ppermute | solution.py:20
  138.0 4.8 %fusion.85 = f32[16,128,128,1]{1,2,3,0:T(8,128)S(1)} fusion(bf16[16,8,128,128]{3,2,1,0:T(8,128)(2,1)} %param.8, bf16[16,8,128,128]{3,2,1,0:T(8,128)(2,1)} %bitcast.291), kind=kOutput, calls=%fused_computation.131 | convolution fusion | flops 536870912 | bytes 9437184 | tf_op jit(solution)/shard_map/rsij,rsjv->riv/dot_general | solution.py:39
  149.4 4.4 %collective-permute-done.15 = bf16[512,128]{1,0:T(8,128)(2,1)S(1)} collective-permute-done((bf16[512,128]{1,0:T(8,128)(2,1)S(1)}, bf16[512,128]{1,0:T(8,128)(2,1)S(1)}, u32[]{:S(2)}, u32[]{:S(2)}) %collective-permute-start.15) | collective-permute-done | bytes 131104 | tf_op jit(solution)/shard_map/ppermute | solution.py:20
  157.0 4.8 %fusion.86 = f32[16,128,128,1]{1,2,3,0:T(8,128)S(1)} fusion(bf16[16,8,128,128]{3,2,1,0:T(8,128)(2,1)} %param.8, bf16[16,8,128,128]{3,2,1,0:T(8,128)(2,1)} %bitcast.292), kind=kOutput, calls=%fused_computation.132 | convolution fusion | flops 536870912 | bytes 9437184 | tf_op jit(solution)/shard_map/rsij,rsjv->riv/dot_general | solution.py:39
  168.7 4.4 %collective-permute-done.17 = bf16[512,128]{1,0:T(8,128)(2,1)S(1)} collective-permute-done((bf16[512,128]{1,0:T(8,128)(2,1)S(1)}, bf16[512,128]{1,0:T(8,128)(2,1)S(1)}, u32[]{:S(2)}, u32[]{:S(2)}) %collective-permute-start.17) | collective-permute-done | bytes 131104 | tf_op jit(solution)/shard_map/ppermute | solution.py:20
  176.3 4.8 %fusion.87 = f32[16,128,128,1]{1,2,3,0:T(8,128)S(1)} fusion(bf16[16,8,128,128]{3,2,1,0:T(8,128)(2,1)} %param.8, bf16[16,8,128,128]{3,2,1,0:T(8,128)(2,1)} %bitcast.293), kind=kOutput, calls=%fused_computation.133 | convolution fusion | flops 536870912 | bytes 9437184 | tf_op jit(solution)/shard_map/rsij,rsjv->riv/dot_general | solution.py:39
  189.0 4.4 %collective-permute-done.19 = bf16[512,128]{1,0:T(8,128)(2,1)S(1)} collective-permute-done((bf16[512,128]{1,0:T(8,128)(2,1)S(1)}, bf16[512,128]{1,0:T(8,128)(2,1)S(1)}, u32[]{:S(2)}, u32[]{:S(2)}) %collective-permute-start.19) | collective-permute-done | bytes 131104 | tf_op jit(solution)/shard_map/ppermute | solution.py:20
  196.6 4.8 %fusion.88 = f32[16,128,128,1]{1,2,3,0:T(8,128)S(1)} fusion(bf16[16,8,128,128]{3,2,1,0:T(8,128)(2,1)} %param.8, bf16[16,8,128,128]{3,2,1,0:T(8,128)(2,1)} %bitcast.294), kind=kOutput, calls=%fused_computation.134 | convolution fusion | flops 536870912 | bytes 9437184 | tf_op jit(solution)/shard_map/rsij,rsjv->riv/dot_general | solution.py:39
  215.8 4.8 %fusion.89 = f32[16,128,128,1]{1,2,3,0:T(8,128)S(1)} fusion(bf16[16,8,128,128]{3,2,1,0:T(8,128)(2,1)} %param.8, bf16[16,8,128,128]{3,2,1,0:T(8,128)(2,1)} %bitcast.295), kind=kOutput, calls=%fused_computation.135 | convolution fusion | flops 536870912 | bytes 9437184 | tf_op jit(solution)/shard_map/rsij,rsjv->riv/dot_general | solution.py:39
  235.3 4.8 %fusion.90 = f32[16,128,128,1]{1,2,3,0:T(8,128)S(1)} fusion(bf16[16,8,128,128]{3,2,1,0:T(8,128)(2,1)} %param.8, bf16[16,8,128,128]{3,2,1,0:T(8,128)(2,1)} %bitcast.284), kind=kOutput, calls=%fused_computation.136 | convolution fusion | flops 536870912 | bytes 9437184 | tf_op jit(solution)/shard_map/rsij,rsjv->riv/dot_general | solution.py:39
  240.2 6.7 %fusion.53 = (bf16[2048,128]{1,0:T(8,128)(2,1)S(1)}, f32[2048,128]{1,0:T(8,128)}) fusion(f32[16,128,128,1]{1,2,3,0:T(8,128)S(1)} %fusion.90, f32[]{:T(128)} %bitcast.38, f32[2048,128]{1,0:T(8,128)S(1)} %copy-done.12, f32[16,128,128,1]{1,2,3,0:T(8,128)S(1)} %copy-done.18, f32[]{:T(128)} %bitcast.31, f32[2048,128]{1,0:T(8,128)S(1)} %get-tuple-element.12, ...), kind=kLoop, calls=%fused_computation.104 | loop fusion | flops 8388608 | bytes 8912932 | tf_op jit(solution)/shard_map/convert_element_type | solution.py:79
  249.1 8.6 %collective-permute-done.24 = bf16[32,2048]{0,1:T(8,128)(2,1)S(1)} collective-permute-done((bf16[32,2048]{0,1:T(8,128)(2,1)S(1)}, bf16[32,2048]{0,1:T(8,128)(2,1)S(1)}, u32[]{:S(2)}, u32[]{:S(2)}) %collective-permute-start.24) | collective-permute-done | bytes 131104 | tf_op jit(solution)/shard_map/ppermute | solution.py:28
  258.3 139.8 %all-reduce.12 = (f32[32,128]{1,0:T(8,128)S(1)}, f32[32,32]{1,0:T(8,128)S(1)}) all-reduce(f32[32,128]{1,0:T(8,128)S(1)} %fusion.78, f32[32,32]{1,0:T(8,128)S(1)} %fusion.77), channel_id=1, replica_groups=mesh['cuts'=8,'rows'=32] {'rows'}, use_global_device_ids=true, to_apply=%region_3.4 | all-reduce | flops 5120 | bytes 40960 | tf_op jit(solution)/shard_map/psum | solution.py:84
  (164 shorter events, 148.5 us)
Async XLA Ops:
  1.0 7.3 %collective-permute-start = (bf16[512,128]{1,0:T(8,128)(2,1)S(1)}, bf16[512,128]{1,0:T(8,128)(2,1)S(1)}, u32[]{:S(2)}, u32[]{:S(2)}) collective-permute-start(bf16[512,128]{1,0:T(8,128)(2,1)S(1)} %get-tuple-element.41), channel_id=1, source_target_pairs={{0,1},{1,2},{2,3},{3,4},{4,5},{5,6},{6,7},{7,8},{8,9},{9,10},{10,1... | collective-permute-start | bytes 393224 | tf_op jit(solution)/shard_map/ppermute | solution.py:17
  4.8 7.0 %collective-permute-start.1 = (bf16[512,128]{1,0:T(8,128)(2,1)S(1)}, bf16[512,128]{1,0:T(8,128)(2,1)S(1)}, u32[]{:S(2)}, u32[]{:S(2)}) collective-permute-start(bf16[512,128]{1,0:T(8,128)(2,1)S(1)} %get-tuple-element.42), channel_id=1, source_target_pairs={{1,0},{2,1},{3,2},{4,3},{5,4},{6,5},{7,6},{8,7},{9,8},{10,9},{11,1... | collective-permute-start | bytes 393224 | tf_op jit(solution)/shard_map/ppermute | solution.py:20
  21.1 6.3 %collective-permute-start.2 = (bf16[512,128]{1,0:T(8,128)(2,1)S(1)}, bf16[512,128]{1,0:T(8,128)(2,1)S(1)}, u32[]{:S(2)}, u32[]{:S(2)}) collective-permute-start(bf16[512,128]{1,0:T(8,128)(2,1)S(1)} %get-tuple-element.39), channel_id=1, source_target_pairs={{0,1},{1,2},{2,3},{3,4},{4,5},{5,6},{6,7},{7,8},{8,9},{9,10},{10,1... | collective-permute-start | bytes 393224 | tf_op jit(solution)/shard_map/ppermute | solution.py:17
  24.9 8.0 %collective-permute-start.3 = (bf16[512,128]{1,0:T(8,128)(2,1)S(1)}, bf16[512,128]{1,0:T(8,128)(2,1)S(1)}, u32[]{:S(2)}, u32[]{:S(2)}) collective-permute-start(bf16[512,128]{1,0:T(8,128)(2,1)S(1)} %get-tuple-element.40), channel_id=1, source_target_pairs={{1,0},{2,1},{3,2},{4,3},{5,4},{6,5},{7,6},{8,7},{9,8},{10,9},{11,1... | collective-permute-start | bytes 393224 | tf_op jit(solution)/shard_map/ppermute | solution.py:20
  41.2 7.4 %collective-permute-start.4 = (bf16[512,128]{1,0:T(8,128)(2,1)S(1)}, bf16[512,128]{1,0:T(8,128)(2,1)S(1)}, u32[]{:S(2)}, u32[]{:S(2)}) collective-permute-start(bf16[512,128]{1,0:T(8,128)(2,1)S(1)} %get-tuple-element.37), channel_id=1, source_target_pairs={{0,1},{1,2},{2,3},{3,4},{4,5},{5,6},{6,7},{7,8},{8,9},{9,10},{10,1... | collective-permute-start | bytes 393224 | tf_op jit(solution)/shard_map/ppermute | solution.py:17
  46.1 6.9 %collective-permute-start.5 = (bf16[512,128]{1,0:T(8,128)(2,1)S(1)}, bf16[512,128]{1,0:T(8,128)(2,1)S(1)}, u32[]{:S(2)}, u32[]{:S(2)}) collective-permute-start(bf16[512,128]{1,0:T(8,128)(2,1)S(1)} %get-tuple-element.38), channel_id=1, source_target_pairs={{1,0},{2,1},{3,2},{4,3},{5,4},{6,5},{7,6},{8,7},{9,8},{10,9},{11,1... | collective-permute-start | bytes 393224 | tf_op jit(solution)/shard_map/ppermute | solution.py:20
  62.3 6.4 %collective-permute-start.6 = (bf16[512,128]{1,0:T(8,128)(2,1)S(1)}, bf16[512,128]{1,0:T(8,128)(2,1)S(1)}, u32[]{:S(2)}, u32[]{:S(2)}) collective-permute-start(bf16[512,128]{1,0:T(8,128)(2,1)S(1)} %get-tuple-element.35), channel_id=1, source_target_pairs={{0,1},{1,2},{2,3},{3,4},{4,5},{5,6},{6,7},{7,8},{8,9},{9,10},{10,1... | collective-permute-start | bytes 393224 | tf_op jit(solution)/shard_map/ppermute | solution.py:17
  66.2 6.9 %collective-permute-start.7 = (bf16[512,128]{1,0:T(8,128)(2,1)S(1)}, bf16[512,128]{1,0:T(8,128)(2,1)S(1)}, u32[]{:S(2)}, u32[]{:S(2)}) collective-permute-start(bf16[512,128]{1,0:T(8,128)(2,1)S(1)} %get-tuple-element.36), channel_id=1, source_target_pairs={{1,0},{2,1},{3,2},{4,3},{5,4},{6,5},{7,6},{8,7},{9,8},{10,9},{11,1... | collective-permute-start | bytes 393224 | tf_op jit(solution)/shard_map/ppermute | solution.py:20
  81.4 5.6 %collective-permute-start.8 = (bf16[512,128]{1,0:T(8,128)(2,1)S(1)}, bf16[512,128]{1,0:T(8,128)(2,1)S(1)}, u32[]{:S(2)}, u32[]{:S(2)}) collective-permute-start(bf16[512,128]{1,0:T(8,128)(2,1)S(1)} %get-tuple-element.33), channel_id=1, source_target_pairs={{0,1},{1,2},{2,3},{3,4},{4,5},{5,6},{6,7},{7,8},{8,9},{9,10},{10,1... | collective-permute-start | bytes 393224 | tf_op jit(solution)/shard_map/ppermute | solution.py:17
  84.5 6.9 %collective-permute-start.9 = (bf16[512,128]{1,0:T(8,128)(2,1)S(1)}, bf16[512,128]{1,0:T(8,128)(2,1)S(1)}, u32[]{:S(2)}, u32[]{:S(2)}) collective-permute-start(bf16[512,128]{1,0:T(8,128)(2,1)S(1)} %get-tuple-element.34), channel_id=1, source_target_pairs={{1,0},{2,1},{3,2},{4,3},{5,4},{6,5},{7,6},{8,7},{9,8},{10,9},{11,1... | collective-permute-start | bytes 393224 | tf_op jit(solution)/shard_map/ppermute | solution.py:20
  99.9 5.6 %collective-permute-start.10 = (bf16[512,128]{1,0:T(8,128)(2,1)S(1)}, bf16[512,128]{1,0:T(8,128)(2,1)S(1)}, u32[]{:S(2)}, u32[]{:S(2)}) collective-permute-start(bf16[512,128]{1,0:T(8,128)(2,1)S(1)} %get-tuple-element.31), channel_id=1, source_target_pairs={{0,1},{1,2},{2,3},{3,4},{4,5},{5,6},{6,7},{7,8},{8,9},{9,10},{10,1... | collective-permute-start | bytes 393224 | tf_op jit(solution)/shard_map/ppermute | solution.py:17
  103.1 6.9 %collective-permute-start.11 = (bf16[512,128]{1,0:T(8,128)(2,1)S(1)}, bf16[512,128]{1,0:T(8,128)(2,1)S(1)}, u32[]{:S(2)}, u32[]{:S(2)}) collective-permute-start(bf16[512,128]{1,0:T(8,128)(2,1)S(1)} %get-tuple-element.32), channel_id=1, source_target_pairs={{1,0},{2,1},{3,2},{4,3},{5,4},{6,5},{7,6},{8,7},{9,8},{10,9},{11,1... | collective-permute-start | bytes 393224 | tf_op jit(solution)/shard_map/ppermute | solution.py:20
  127.9 6.9 %collective-permute-start.13 = (bf16[512,128]{1,0:T(8,128)(2,1)S(1)}, bf16[512,128]{1,0:T(8,128)(2,1)S(1)}, u32[]{:S(2)}, u32[]{:S(2)}) collective-permute-start(bf16[512,128]{1,0:T(8,128)(2,1)S(1)} %get-tuple-element.30), channel_id=1, source_target_pairs={{1,0},{2,1},{3,2},{4,3},{5,4},{6,5},{7,6},{8,7},{9,8},{10,9},{11,1... | collective-permute-start | bytes 393224 | tf_op jit(solution)/shard_map/ppermute | solution.py:20
  143.0 6.4 %collective-permute-start.14 = (bf16[512,128]{1,0:T(8,128)(2,1)S(1)}, bf16[512,128]{1,0:T(8,128)(2,1)S(1)}, u32[]{:S(2)}, u32[]{:S(2)}) collective-permute-start(bf16[512,128]{1,0:T(8,128)(2,1)S(1)} %get-tuple-element.27), channel_id=1, source_target_pairs={{0,1},{1,2},{2,3},{3,4},{4,5},{5,6},{6,7},{7,8},{8,9},{9,10},{10,1... | collective-permute-start | bytes 393224 | tf_op jit(solution)/shard_map/ppermute | solution.py:17
  146.9 6.9 %collective-permute-start.15 = (bf16[512,128]{1,0:T(8,128)(2,1)S(1)}, bf16[512,128]{1,0:T(8,128)(2,1)S(1)}, u32[]{:S(2)}, u32[]{:S(2)}) collective-permute-start(bf16[512,128]{1,0:T(8,128)(2,1)S(1)} %get-tuple-element.28), channel_id=1, source_target_pairs={{1,0},{2,1},{3,2},{4,3},{5,4},{6,5},{7,6},{8,7},{9,8},{10,9},{11,1... | collective-permute-start | bytes 393224 | tf_op jit(solution)/shard_map/ppermute | solution.py:20
  162.2 6.5 %collective-permute-start.16 = (bf16[512,128]{1,0:T(8,128)(2,1)S(1)}, bf16[512,128]{1,0:T(8,128)(2,1)S(1)}, u32[]{:S(2)}, u32[]{:S(2)}) collective-permute-start(bf16[512,128]{1,0:T(8,128)(2,1)S(1)} %get-tuple-element.25), channel_id=1, source_target_pairs={{0,1},{1,2},{2,3},{3,4},{4,5},{5,6},{6,7},{7,8},{8,9},{9,10},{10,1... | collective-permute-start | bytes 393224 | tf_op jit(solution)/shard_map/ppermute | solution.py:17
  166.2 6.9 %collective-permute-start.17 = (bf16[512,128]{1,0:T(8,128)(2,1)S(1)}, bf16[512,128]{1,0:T(8,128)(2,1)S(1)}, u32[]{:S(2)}, u32[]{:S(2)}) collective-permute-start(bf16[512,128]{1,0:T(8,128)(2,1)S(1)} %get-tuple-element.26), channel_id=1, source_target_pairs={{1,0},{2,1},{3,2},{4,3},{5,4},{6,5},{7,6},{8,7},{9,8},{10,9},{11,1... | collective-permute-start | bytes 393224 | tf_op jit(solution)/shard_map/ppermute | solution.py:20
  182.5 6.5 %collective-permute-start.18 = (bf16[512,128]{1,0:T(8,128)(2,1)S(1)}, bf16[512,128]{1,0:T(8,128)(2,1)S(1)}, u32[]{:S(2)}, u32[]{:S(2)}) collective-permute-start(bf16[512,128]{1,0:T(8,128)(2,1)S(1)} %get-tuple-element.23), channel_id=1, source_target_pairs={{0,1},{1,2},{2,3},{3,4},{4,5},{5,6},{6,7},{7,8},{8,9},{9,10},{10,1... | collective-permute-start | bytes 393224 | tf_op jit(solution)/shard_map/ppermute | solution.py:17
  186.5 6.9 %collective-permute-start.19 = (bf16[512,128]{1,0:T(8,128)(2,1)S(1)}, bf16[512,128]{1,0:T(8,128)(2,1)S(1)}, u32[]{:S(2)}, u32[]{:S(2)}) collective-permute-start(bf16[512,128]{1,0:T(8,128)(2,1)S(1)} %get-tuple-element.24), channel_id=1, source_target_pairs={{1,0},{2,1},{3,2},{4,3},{5,4},{6,5},{7,6},{8,7},{9,8},{10,9},{11,1... | collective-permute-start | bytes 393224 | tf_op jit(solution)/shard_map/ppermute | solution.py:20
  201.7 6.5 %collective-permute-start.20 = (bf16[512,128]{1,0:T(8,128)(2,1)S(1)}, bf16[512,128]{1,0:T(8,128)(2,1)S(1)}, u32[]{:S(2)}, u32[]{:S(2)}) collective-permute-start(bf16[512,128]{1,0:T(8,128)(2,1)S(1)} %get-tuple-element.21), channel_id=1, source_target_pairs={{0,1},{1,2},{2,3},{3,4},{4,5},{5,6},{6,7},{7,8},{8,9},{9,10},{10,1... | collective-permute-start | bytes 393224 | tf_op jit(solution)/shard_map/ppermute | solution.py:17
  205.7 6.9 %collective-permute-start.21 = (bf16[512,128]{1,0:T(8,128)(2,1)S(1)}, bf16[512,128]{1,0:T(8,128)(2,1)S(1)}, u32[]{:S(2)}, u32[]{:S(2)}) collective-permute-start(bf16[512,128]{1,0:T(8,128)(2,1)S(1)} %get-tuple-element.22), channel_id=1, source_target_pairs={{1,0},{2,1},{3,2},{4,3},{5,4},{6,5},{7,6},{8,7},{9,8},{10,9},{11,1... | collective-permute-start | bytes 393224 | tf_op jit(solution)/shard_map/ppermute | solution.py:20
  221.1 6.5 %collective-permute-start.22 = (bf16[512,128]{1,0:T(8,128)(2,1)S(1)}, bf16[512,128]{1,0:T(8,128)(2,1)S(1)}, u32[]{:S(2)}, u32[]{:S(2)}) collective-permute-start(bf16[512,128]{1,0:T(8,128)(2,1)S(1)} %get-tuple-element.19), channel_id=1, source_target_pairs={{0,1},{1,2},{2,3},{3,4},{4,5},{5,6},{6,7},{7,8},{8,9},{9,10},{10,1... | collective-permute-start | bytes 393224 | tf_op jit(solution)/shard_map/ppermute | solution.py:17
  225.2 6.9 %collective-permute-start.23 = (bf16[512,128]{1,0:T(8,128)(2,1)S(1)}, bf16[512,128]{1,0:T(8,128)(2,1)S(1)}, u32[]{:S(2)}, u32[]{:S(2)}) collective-permute-start(bf16[512,128]{1,0:T(8,128)(2,1)S(1)} %get-tuple-element.20), channel_id=1, source_target_pairs={{1,0},{2,1},{3,2},{4,3},{5,4},{6,5},{7,6},{8,7},{9,8},{10,9},{11,1... | collective-permute-start | bytes 393224 | tf_op jit(solution)/shard_map/ppermute | solution.py:20
  247.1 10.6 %collective-permute-start.24 = (bf16[32,2048]{0,1:T(8,128)(2,1)S(1)}, bf16[32,2048]{0,1:T(8,128)(2,1)S(1)}, u32[]{:S(2)}, u32[]{:S(2)}) collective-permute-start(bf16[32,2048]{0,1:T(8,128)(2,1)S(1)} %slice_bitcast_fusion), channel_id=1, source_target_pairs={{0,32},{32,64},{64,96},{96,128},{128,160},{160,192},{192,224},{1,3... | collective-permute-start | bytes 393224 | tf_op jit(solution)/shard_map/ppermute | solution.py:28
  (24 other events, 294.6 us)
where the time goes:
time: 407 us; the launch traced here: 406 us
  blocking collectives  140 us (34%)
  waiting for transfers between devices  73.3 us (18%)
  starting transfers between devices  63.8 us (16%)
  matrix products  59.4 us (15%)
  local copies, waits for them, and re-layouts  40.3 us (10%)
  other arithmetic  27.5 us (7%)
    psum x1, blocking collectives, body(): gram_sum, cross_sum = lax.psum((gram_part, cross_part), 'rows')  140 us
    dot_general x12, matrix products, gather_product(): jnp.einsum('rsij,rsjv->riv', blocks, padded_source[picked], preferred_ele...  57.4 us
    ppermute x12, waiting for transfers between devices, with_halo(): lax.ppermute(lax.slice_in_dim(block, 0, width, axis=dim), axis, backward)  52.7 us
    ppermute x12, starting transfers between devices, with_halo(): lax.ppermute(lax.slice_in_dim(block, block.shape[dim] - width, None, axis...  45.9 us
    gather x12, local copies, waits for them, and re-layouts, gather_product(): padded_source[picked]  36.9 us
    ppermute x12, starting transfers between devices, with_halo(): lax.ppermute(lax.slice_in_dim(block, 0, width, axis=dim), axis, backward)  15.9 us
    ppermute x12, waiting for transfers between devices, with_halo(): lax.ppermute(lax.slice_in_dim(block, block.shape[dim] - width, None, axis...  12.1 us
    ppermute x1, waiting for transfers between devices, passed_along(): lax.ppermute(value, axis, [(source, source + steps) for source in range(l...  8.57 us
  transfers between devices with their start and end apart: 25, of which 24 were waited for; matrix products, arithmetic and copies ran while one was open for 0% of the time, Pallas kernels for 0%

commit v1 on v0

v1 whole, which is shorter than its diff:
```python
import functools

import jax
import jax.numpy as jnp
from jax import lax
from jax.experimental import pallas as pl
from jax.experimental.pallas import tpu as pltpu
from jax.sharding import PartitionSpec as P

BS = 128
MAXB = 8
W = 4
DEG = 6
PASSES = 2
NB = 32
RB = 16
HALO = W * BS
OWN = RB * BS
QUADS = RB // W
WIDE = 3 * W * BS
MESH = pl.DeviceIdType.MESH
F32 = jnp.float32
BF16 = jnp.bfloat16


def dot(a, b):
    return jnp.dot(a, b, preferred_element_type=F32)


def tdot(a, b):
    return lax.dot_general(a, b, (((0,), (0,)), ((), ())), preferred_element_type=F32)


def kernel(
    nz,
    nx,
    ncut,
    vec,
    blocks,
    cols,
    counts,
    lower,
    upper,
    coeffs,
    out,
    stage0,
    stage1,
    stage2,
    stage3,
    dense,
    vbuf,
    ybuf,
    total,
    start,
    packed,
    arrived,
    acc,
    part,
    zin,
    xin,
    mid,
    full,
    block_sem,
    vec_sem,
    send_sem,
    recv_sem,
    edge_sem,
    zsend,
    zrecv,
    xsend,
    xrecv,
    gsend,
    grecv,
):
    stages = (stage0, stage1, stage2, stage3)
    row = lax.axis_index("rows")
    cut = lax.axis_index("cuts")
    nrow = nz * nx
    z = lax.rem(row, nz)
    x = lax.div(row, nz)
    low = lax.rem(row + nrow - 1, nrow)
    high = lax.rem(row + 1, nrow)
    after = lax.rem(cut + 1, ncut)
    before = lax.rem(cut + ncut - 1, ncut)
    zpeers = [x * nz + lax.rem(z + o, nz) for o in range(1, nz)]
    xpeers = [lax.rem(x + o, nx) * nz + z for o in range(1, nx)]

    vec_copy = pltpu.make_async_copy(vec, start, vec_sem)
    vec_copy.start()
    block_copies = []
    for q in range(QUADS):
        copy = pltpu.make_async_copy(
            blocks.at[pl.ds(q * W * MAXB, W * MAXB)],
            stages[q].at[pl.ds(0, W * MAXB)],
            block_sem.at[q],
        )
        copy.start()
        block_copies.append(copy)

    barrier = pltpu.get_barrier_semaphore()
    greeted = 0
    for other in [low, high, *zpeers, *xpeers]:
        pl.semaphore_signal(barrier, inc=1, device_id=(cut, other), device_id_type=MESH)
        greeted += 1
    for other in (before, after):
        pl.semaphore_signal(barrier, inc=1, device_id=(other, row), device_id_type=MESH)
        greeted += 1

    for q in range(QUADS):
        dense[q] = jnp.zeros((W * BS, WIDE), BF16)
        stages[q][W * MAXB] = jnp.zeros((BS, BS), BF16)
    centre = (lower[0] + upper[0]) * 0.5
    half = (upper[0] - lower[0]) * 0.5
    inverse = 1.0 / half

    pl.semaphore_wait(barrier, greeted)

    def to_low(src, slot):
        return pltpu.make_async_remote_copy(
            src_ref=src,
            dst_ref=vbuf.at[slot, pl.ds(HALO + OWN, HALO)],
            send_sem=send_sem.at[0, slot],
            recv_sem=recv_sem.at[1, slot],
            device_id=(cut, low),
            device_id_type=MESH,
        )

    def to_high(src, slot):
        return pltpu.make_async_remote_copy(
            src_ref=src,
            dst_ref=vbuf.at[slot, pl.ds(0, HALO)],
            send_sem=send_sem.at[1, slot],
            recv_sem=recv_sem.at[0, slot],
            device_id=(cut, high),
            device_id_type=MESH,
        )

    def low_edge(slot):
        return to_low(vbuf.at[slot, pl.ds(HALO, HALO)], slot)

    def high_edge(slot):
        return to_high(vbuf.at[slot, pl.ds(OWN, HALO)], slot)

    to_low(vec.at[pl.ds(0, HALO)], 0).start()
    to_high(vec.at[pl.ds(OWN - HALO, HALO)], 0).start()

    vec_copy.wait()
    vbuf[0, pl.ds(HALO, OWN)] = start[...]
    first = start[...].astype(F32)
    ybuf[0] = first
    ybuf[1] = jnp.zeros((OWN, BS), F32)
    total[...] = coeffs[0, 0] * first

    for q in range(QUADS):
        block_copies[q].wait()

        def place(i, carry, q=q):
            r = q * W + i
            base = row * RB + r - W
            live = counts[r]
            near = [jnp.where(s < live, cols[s, r] - base, -1) for s in range(MAXB)]
            for d in range(2 * W + 1):
                slot = jnp.int32(W * MAXB)
                for s in range(MAXB):
                    slot = jnp.where(near[s] == d, i * MAXB + s, slot)
                rows = pl.ds(pl.multiple_of(i * BS, BS), BS)
                lanes = pl.ds(pl.multiple_of((i + d) * BS, BS), BS)
                dense[q, rows, lanes] = stages[q][slot]
            return carry

        lax.fori_loop(0, W, place, 0)

    def step(k, carry):
        now = lax.rem(k, 2)
        new = 1 - now
        term = lax.rem(k, DEG)
        opening = term == 0
        closing = term == DEG - 1
        scale = jnp.where(opening, 1.0, 2.0) * inverse
        shift = scale * centre
        keep = jnp.where(opening, 0.0, 1.0)
        weight = coeffs[0, term + 1]
        first_weight = coeffs[0, 0]

        def finish(at, count, product):
            rows = pl.ds(at, count)
            upcoming = (
                scale * product - shift * ybuf[now, rows] - keep * ybuf[new, rows]
            )
            summed = total[rows] + weight * upcoming
            value = jnp.where(closing, summed, upcoming)
            total[rows] = jnp.where(closing, first_weight * summed, summed)
            ybuf[new, rows] = value
            vbuf[new, pl.ds(HALO + at, count)] = value.astype(BF16)

        half_rows = 2 * BS
        wide = (2 * W + 2) * BS
        def inner(n, carry):
            q, j = 1 + lax.div(n, 2), lax.rem(n, 2)
            at = pl.multiple_of(HALO + n * half_rows, half_rows)
            within = pl.multiple_of(j * half_rows, half_rows)
            product = dot(
                dense[q, pl.ds(within, half_rows), pl.ds(within, wide)],
                vbuf[now, pl.ds(at, wide)],
            )
            finish(at, half_rows, product)
            return carry

        lax.fori_loop(0, 4, inner, 0)
        acc[0] = dot(dense[0, :, HALO:], vbuf[now, pl.ds(HALO, 2 * HALO)])
        acc[1] = dot(dense[QUADS - 1, :, : 2 * HALO], vbuf[now, pl.ds(OWN - HALO, 2 * HALO)])

        @pl.when(k > 0)
        def _():
            low_edge(new).wait_send()
            high_edge(new).wait_send()

        to_high(vbuf.at[now, pl.ds(OWN, HALO)], now).wait_recv()
        finish(0, HALO, acc[0] + dot(dense[0, :, :HALO], vbuf[now, pl.ds(0, HALO)]))

        @pl.when(k < PASSES * DEG - 1)
        def _():
            low_edge(new).start()

        to_low(vbuf.at[now, pl.ds(HALO, HALO)], now).wait_recv()
        finish(
            OWN - HALO,
            HALO,
            acc[1] + dot(dense[QUADS - 1, :, 2 * HALO :], vbuf[now, pl.ds(HALO + OWN, HALO)]),
        )

        @pl.when(k < PASSES * DEG - 1)
        def _():
            high_edge(new).start()

        return carry

    lax.fori_loop(0, PASSES * DEG, step, 0)
    last = (PASSES * DEG) % 2
    low_edge(1 - last).wait_send()
    high_edge(1 - last).wait_send()

    lane = lax.broadcasted_iota(jnp.int32, (HALO, BS), 1)
    strip = jnp.zeros((HALO, BS), F32)
    for g in range(W):
        turned = pltpu.roll(ybuf[last, g * HALO : (g + 1) * HALO], (NB * (g + 1)) % BS, 1)
        strip = jnp.where(lane // NB == g, turned, strip)
    packed[...] = strip.astype(BF16)
    edge = pltpu.make_async_remote_copy(
        src_ref=packed,
        dst_ref=arrived,
        send_sem=edge_sem.at[0],
        recv_sem=edge_sem.at[1],
        device_id=(after, row),
        device_id_type=MESH,
    )
    edge.start()
    edge.wait()
    @pl.when(cut == 0)
    def _():
        arrived[...] = jnp.zeros((HALO, BS), BF16)

    boundary = arrived[...]
    cross = jnp.zeros((NB, BS), F32)
    for g in range(W):
        mine = vbuf[last, pl.ds(HALO + g * HALO, HALO)]
        cross = cross + tdot(boundary, mine)[g * NB : (g + 1) * NB]
    square = tdot(boundary, boundary)
    gram = jnp.zeros((NB, BS), F32)
    for g in range(W):
        rows = square[g * NB : (g + 1) * NB]
        gram = gram + (pltpu.roll(rows, (BS - NB * g) % BS, 1) if g else rows)
    part[0:NB] = cross
    part[NB : 2 * NB] = gram

    piece = 2 * NB // nz
    mine = pl.ds(pl.multiple_of(z * piece, piece), piece)
    copies = []
    for o in range(1, nz):
        theirs = pl.multiple_of(lax.rem(z + o, nz) * piece, piece)
        copies.append(
            pltpu.make_async_remote_copy(
                src_ref=part.at[pl.ds(theirs, piece)],
                dst_ref=zin.at[o - 1],
                send_sem=zsend.at[o - 1],
                recv_sem=zrecv.at[o - 1],
                device_id=(cut, zpeers[o - 1]),
                device_id_type=MESH,
            )
        )
        copies[-1].start()
    summed = part[mine]
    for o in range(1, nz):
        copies[o - 1].wait()
        summed = summed + zin[o - 1]
    mid[...] = summed
    copies = []
    for o in range(1, nx):
        copies.append(
            pltpu.make_async_remote_copy(
                src_ref=mid,
                dst_ref=xin.at[o - 1],
                send_sem=xsend.at[o - 1],
                recv_sem=xrecv.at[o - 1],
                device_id=(cut, xpeers[o - 1]),
                device_id_type=MESH,
            )
        )
        copies[-1].start()
    for o in range(1, nx):
        copies[o - 1].wait()
        summed = summed + xin[o - 1]
    full[mine] = summed
    copies = []
    for o in range(1, nz):
        copies.append(
            pltpu.make_async_remote_copy(
                src_ref=full.at[mine],
                dst_ref=full.at[mine],
                send_sem=gsend.at[o - 1],
                recv_sem=grecv.at[o - 1],
                device_id=(cut, zpeers[o - 1]),
                device_id_type=MESH,
            )
        )
        copies[-1].start()
    for copy in copies:
        copy.wait()

    across = lax.broadcasted_iota(jnp.int32, (NB, BS), 1)
    down = lax.broadcasted_iota(jnp.int32, (NB, BS), 0)
    right = full[0:NB]
    left = full[NB : 2 * NB] + jnp.where(across == down, 1.0, 0.0)
    for j in range(NB):
        column = left[:, j : j + 1]
        pivot = 1.0 / left[j : j + 1, j : j + 1]
        lrow = left[j : j + 1] * pivot
        rrow = right[j : j + 1] * pivot
        left = jnp.where(down == j, lrow, left - column * lrow)
        right = jnp.where(down == j, rrow, right - column * rrow)
    solved = right.astype(BF16).astype(F32)
    for g in range(W):
        above_rows = [jnp.zeros((NB, BS), F32)] * g
        below_rows = [jnp.zeros((NB, BS), F32)] * (W - 1 - g)
        spread = jnp.concatenate([*above_rows, solved, *below_rows], axis=0).astype(BF16)
        correction = dot(boundary, spread)
        rows = pl.ds(g * HALO, HALO)
        out[rows] = (ybuf[last, rows] - correction).astype(BF16)


def body(nz, nx, ncut, vectors, blocks, block_cols, counts, lower_end, upper_end, coeffs):
    blocks = blocks.reshape(RB * MAXB, BS, BS)
    hbm = pl.BlockSpec(memory_space=pl.ANY)
    smem = pl.BlockSpec(memory_space=pltpu.SMEM)
    stage = pltpu.VMEM((W * MAXB + 1, BS, BS), BF16)
    dma = pltpu.SemaphoreType.DMA
    piece = 2 * NB // nz
    return pl.pallas_call(
        functools.partial(kernel, nz, nx, ncut),
        out_shape=jax.ShapeDtypeStruct((OWN, BS), BF16),
        in_specs=[hbm, hbm, smem, smem, smem, smem, smem],
        out_specs=pl.BlockSpec(memory_space=pltpu.VMEM),
        scratch_shapes=[
            stage,
            stage,
            stage,
            stage,
            pltpu.VMEM((QUADS, HALO, WIDE), BF16),
            pltpu.VMEM((2, OWN + 2 * HALO, BS), BF16),
            pltpu.VMEM((2, OWN, BS), F32),
            pltpu.VMEM((OWN, BS), F32),
            pltpu.VMEM((OWN, BS), BF16),
            pltpu.VMEM((HALO, BS), BF16),
            pltpu.VMEM((HALO, BS), BF16),
            pltpu.VMEM((2, HALO, BS), F32),
            pltpu.VMEM((2 * NB, BS), F32),
            pltpu.VMEM((nz - 1, piece, BS), F32),
            pltpu.VMEM((nx - 1, piece, BS), F32),
            pltpu.VMEM((piece, BS), F32),
            pltpu.VMEM((2 * NB, BS), F32),
            dma((QUADS,)),
            dma,
            dma((2, 2)),
            dma((2, 2)),
            dma((2,)),
            dma((nz - 1,)),
            dma((nz - 1,)),
            dma((nx - 1,)),
            dma((nx - 1,)),
            dma((nz - 1,)),
            dma((nz - 1,)),
        ],
        compiler_params=pltpu.CompilerParams(
            collective_id=0, has_side_effects=True, vmem_limit_bytes=60 * 1024 * 1024
        ),
    )(vectors, blocks, block_cols.T, counts, lower_end, upper_end, coeffs)


def solution(mesh):
    rows = mesh.shape["rows"]
    nx = 4 if rows == 32 else 2
    return jax.shard_map(
        functools.partial(body, rows // nx, nx, mesh.shape["cuts"]),
        mesh=mesh,
        in_specs=(
            P("rows", "cuts"),
            P("rows", None, None, None),
            P("rows", None),
            P("rows"),
            P("cuts"),
            P("cuts"),
            P("cuts", None),
        ),
        out_specs=P("rows", "cuts"),
        check_vma=False,
    )
```

time: 407 us -> 108 us (0.27)
  blocking collectives: 140 us -> 0 us
  Pallas kernels: 0 us -> 104 us
  waiting for transfers between devices: 73.3 us -> 0 us
  starting transfers between devices: 63.8 us -> 0 us
  matrix products: 59.4 us -> 0 us
  local copies, waits for them, and re-layouts: 40.3 us -> 1.87 us
  other arithmetic: 27.5 us -> 0 us
    psum x1 -> x0, blocking collectives: 140 us -> none  [body(): gram_sum, cross_sum = lax.psum((gram_part, cross_part), 'rows')]
    pallas_call x0 -> x1, Pallas kernels: none -> 104 us  [body(): pl.pallas_call(functools.partial(kernel, nz, nx, ncut), out_shape=jax.Sha...]
    ppermute x25 -> x0, waiting for transfers between devices: 73.3 us -> none  [the longest x12 52.7 us: with_halo(): lax.ppermute(lax.slice_in_dim(block, 0, width, axis=dim), axis, backward)]
    ppermute x25 -> x0, starting transfers between devices: 63.8 us -> none  [the longest x12 45.9 us: with_halo(): lax.ppermute(lax.slice_in_dim(block, block.shape[dim] - width, None, axis...]
    dot_general x15 -> x0, matrix products: 59 us -> none  [the longest x12 57.4 us: gather_product(): jnp.einsum('rsij,rsjv->riv', blocks, padded_source[picked], preferred_ele...]
    gather x12 -> x0, local copies, waits for them, and re-layouts: 36.9 us -> none  [gather_product(): padded_source[picked]]
    convert_element_type x12 -> x0, other arithmetic: 18.5 us -> none  [the longest x1 6.69 us: body(): previous.astype(jnp.bfloat16)]
    another operation x5 -> x0, other arithmetic: 6.68 us -> none  [the longest x3 3.59 us: body(): factor = jnp.linalg.cholesky(gram_sum)]
  transfers between devices with their start and end apart: 25 -> 0, of which waited for: 24 -> 0; matrix products, arithmetic and copies ran while one was open for 0% -> 0% of each run, Pallas kernels for 0% -> 0%
where the time goes in v1:
time: 108 us; the launch traced here: 107 us
  Pallas kernels  104 us (96%)
  local copies, waits for them, and re-layouts  1.87 us (2%)
  between operations  1.3 us (1%)
    pallas_call x1, Pallas kernels, body(): pl.pallas_call(functools.partial(kernel, nz, nx, ncut), out_shape=jax.Sha...  104 us

profile of v1, /device:TPU:8, one launch (start us, length us, event | category | flops | bytes accessed | tf_op | source)
XLA Modules:
  0.0 106.8 jit_solution(9294314031613290420)
XLA Ops:
  1.3 103.7 %shard_map.73 = bf16[2048,128]{1,0:T(8,128)(2,1)} custom-call(bf16[2048,128]{1,0:T(8,128)(2,1)} %vec.1, bf16[128,128,128]{2,1,0:T(8,128)(2,1)} %bitcast.2, s32[8,16]{1,0:T(8,128)} %bitcast.3, s32[16]{0:T(128)} %counts.1, f32[1]{0:T(128)S(6)} %copy.9.lower, f32[1]{0:T(128)S(6)} %copy.10.upper, f32[1,7]{1,0:T(1,128)} %coeffs.1), custom_call_target="tpu_custom_call" | custom-call | tf_op jit(solution)/shard_map/pallas_call | solution.py:358
  105.0 1.9 %copy.11 = bf16[2048,128]{1,0:T(8,128)(2,1)} copy(bf16[2048,128]{1,0:T(8,128)(2,1)} %shard_map.73) | data formatting | bytes 1048576

commit v2 on v1

--- a/solution.py
+++ b/solution.py
@@ -15,6 +15,7 @@
 NB = 32
 RB = 16
 HALO = W * BS
+PIECE = HALO // 2
 OWN = RB * BS
 QUADS = RB // W
 WIDE = 3 * W * BS
@@ -37,12 +38,17 @@
     ncut,
     vec,
     blocks,
+    cols_in,
+    counts_in,
+    lower_in,
+    upper_in,
+    coeffs_in,
+    out,
     cols,
     counts,
     lower,
     upper,
     coeffs,
-    out,
     stage0,
     stage1,
     stage2,
@@ -55,22 +61,28 @@
     packed,
     arrived,
     acc,
-    part,
-    zin,
-    xin,
-    mid,
-    full,
+    gpart,
+    gzin,
+    gmid,
+    gxin,
+    cpart,
+    czin,
+    cmid,
+    cxin,
+    small_sem,
     block_sem,
     vec_sem,
     send_sem,
     recv_sem,
     edge_sem,
-    zsend,
-    zrecv,
-    xsend,
-    xrecv,
-    gsend,
-    grecv,
+    gzsend,
+    gzrecv,
+    gxsend,
+    gxrecv,
+    czsend,
+    czrecv,
+    cxsend,
+    cxrecv,
 ):
     stages = (stage0, stage1, stage2, stage3)
     row = lax.axis_index("rows")
@@ -87,6 +99,12 @@
 
     vec_copy = pltpu.make_async_copy(vec, start, vec_sem)
     vec_copy.start()
+    small = []
+    for n, (src, dst) in enumerate(
+        ((lower_in, lower), (upper_in, upper), (coeffs_in, coeffs), (cols_in, cols), (counts_in, counts))
+    ):
+        small.append(pltpu.make_async_copy(src, dst, small_sem.at[n]))
+        small[-1].start()
     block_copies = []
     for q in range(QUADS):
         copy = pltpu.make_async_copy(
@@ -109,40 +127,43 @@
     for q in range(QUADS):
         dense[q] = jnp.zeros((W * BS, WIDE), BF16)
         stages[q][W * MAXB] = jnp.zeros((BS, BS), BF16)
+    for copy in small:
+        copy.wait()
     centre = (lower[0] + upper[0]) * 0.5
     half = (upper[0] - lower[0]) * 0.5
     inverse = 1.0 / half
 
     pl.semaphore_wait(barrier, greeted)
 
-    def to_low(src, slot):
+    def to_low(src, slot, p):
         return pltpu.make_async_remote_copy(
             src_ref=src,
-            dst_ref=vbuf.at[slot, pl.ds(HALO + OWN, HALO)],
-            send_sem=send_sem.at[0, slot],
-            recv_sem=recv_sem.at[1, slot],
+            dst_ref=vbuf.at[slot, pl.ds(HALO + OWN + p * PIECE, PIECE)],
+            send_sem=send_sem.at[0, slot, p],
+            recv_sem=recv_sem.at[1, slot, p],
             device_id=(cut, low),
             device_id_type=MESH,
         )
 
-    def to_high(src, slot):
+    def to_high(src, slot, p):
         return pltpu.make_async_remote_copy(
             src_ref=src,
-            dst_ref=vbuf.at[slot, pl.ds(0, HALO)],
-            send_sem=send_sem.at[1, slot],
-            recv_sem=recv_sem.at[0, slot],
+            dst_ref=vbuf.at[slot, pl.ds(p * PIECE, PIECE)],
+            send_sem=send_sem.at[1, slot, p],
+            recv_sem=recv_sem.at[0, slot, p],
             device_id=(cut, high),
             device_id_type=MESH,
         )
 
-    def low_edge(slot):
-        return to_low(vbuf.at[slot, pl.ds(HALO, HALO)], slot)
-
-    def high_edge(slot):
-        return to_high(vbuf.at[slot, pl.ds(OWN, HALO)], slot)
-
-    to_low(vec.at[pl.ds(0, HALO)], 0).start()
-    to_high(vec.at[pl.ds(OWN - HALO, HALO)], 0).start()
+    def low_edge(slot, p):
+        return to_low(vbuf.at[slot, pl.ds(HALO + p * PIECE, PIECE)], slot, p)
+
+    def high_edge(slot, p):
+        return to_high(vbuf.at[slot, pl.ds(OWN + p * PIECE, PIECE)], slot, p)
+
+    for p in (0, 1):
+        to_high(vec.at[pl.ds(OWN - HALO + p * PIECE, PIECE)], 0, p).start()
+        to_low(vec.at[pl.ds(p * PIECE, PIECE)], 0, p).start()
 
     vec_copy.wait()
     vbuf[0, pl.ds(HALO, OWN)] = start[...]
@@ -212,33 +233,47 @@
 
         @pl.when(k > 0)
         def _():
-            low_edge(new).wait_send()
-            high_edge(new).wait_send()
-
-        to_high(vbuf.at[now, pl.ds(OWN, HALO)], now).wait_recv()
-        finish(0, HALO, acc[0] + dot(dense[0, :, :HALO], vbuf[now, pl.ds(0, HALO)]))
-
-        @pl.when(k < PASSES * DEG - 1)
-        def _():
-            low_edge(new).start()
-
-        to_low(vbuf.at[now, pl.ds(HALO, HALO)], now).wait_recv()
-        finish(
-            OWN - HALO,
-            HALO,
-            acc[1] + dot(dense[QUADS - 1, :, 2 * HALO :], vbuf[now, pl.ds(HALO + OWN, HALO)]),
-        )
-
-        @pl.when(k < PASSES * DEG - 1)
-        def _():
-            high_edge(new).start()
+            for p in (0, 1):
+                low_edge(new, p).wait_send()
+                high_edge(new, p).wait_send()
+
+        more = k < PASSES * DEG - 1
+        for p in (0, 1):
+            low_edge(now, p).wait_recv()
+            inside = slice(p * PIECE, (p + 1) * PIECE)
+            deep = (p + 1) * PIECE
+            finish(
+                OWN - HALO + p * PIECE,
+                PIECE,
+                acc[1, inside]
+                + dot(dense[QUADS - 1, inside, 2 * HALO : 2 * HALO + deep], vbuf[now, pl.ds(HALO + OWN, deep)]),
+            )
+
+            @pl.when(more)
+            def _(p=p):
+                high_edge(new, p).start()
+
+        for p in (0, 1):
+            high_edge(now, p).wait_recv()
+        for p in (0, 1):
+            inside = slice(p * PIECE, (p + 1) * PIECE)
+            finish(
+                p * PIECE,
+                PIECE,
+                acc[0, inside] + dot(dense[0, inside, p * PIECE : HALO], vbuf[now, pl.ds(p * PIECE, HALO - p * PIECE)]),
+            )
+
+            @pl.when(more)
+            def _(p=p):
+                low_edge(new, p).start()
 
         return carry
 
     lax.fori_loop(0, PASSES * DEG, step, 0)
     last = (PASSES * DEG) % 2
-    low_edge(1 - last).wait_send()
-    high_edge(1 - last).wait_send()
+    for p in (0, 1):
+        low_edge(1 - last, p).wait_send()
+        high_edge(1 - last, p).wait_send()
 
     lane = lax.broadcasted_iota(jnp.int32, (HALO, BS), 1)
     strip = jnp.zeros((HALO, BS), F32)
@@ -260,84 +295,68 @@
     def _():
         arrived[...] = jnp.zeros((HALO, BS), BF16)
 
+    def share(src, slots, sent, got, peers):
+        copies = []
+        for o, peer in enumerate(peers):
+            copies.append(
+                pltpu.make_async_remote_copy(
+                    src_ref=src,
+                    dst_ref=slots.at[o],
+                    send_sem=sent.at[o],
+                    recv_sem=got.at[o],
+                    device_id=(cut, peer),
+                    device_id_type=MESH,
+                )
+            )
+            copies[-1].start()
+        return copies
+
+    def collect(copies, own, slots):
+        summed = own
+        for o, copy in enumerate(copies):
+            copy.wait()
+            summed = summed + slots[o]
+        return summed
+
     boundary = arrived[...]
+    square = tdot(boundary, boundary)
+    eight = BS // W // W
+    group = lax.broadcasted_iota(jnp.int32, (eight, BS), 1) // NB
+    gram = jnp.zeros((NB, BS), F32)
+    for g in range(W):
+        rows = square[g * NB : (g + 1) * NB]
+        gram = gram + (pltpu.roll(rows, (BS - NB * g) % BS, 1) if g else rows)
+    tight = jnp.zeros((eight, BS), F32)
+    for g in range(W):
+        rows = gram[g * eight : (g + 1) * eight]
+        tight = jnp.where(group == g, pltpu.roll(rows, NB * g, 1) if g else rows, tight)
+    gpart[...] = tight
+    gram_z = share(gpart, gzin, gzsend, gzrecv, zpeers)
     cross = jnp.zeros((NB, BS), F32)
     for g in range(W):
         mine = vbuf[last, pl.ds(HALO + g * HALO, HALO)]
         cross = cross + tdot(boundary, mine)[g * NB : (g + 1) * NB]
-    square = tdot(boundary, boundary)
-    gram = jnp.zeros((NB, BS), F32)
-    for g in range(W):
-        rows = square[g * NB : (g + 1) * NB]
-        gram = gram + (pltpu.roll(rows, (BS - NB * g) % BS, 1) if g else rows)
-    part[0:NB] = cross
-    part[NB : 2 * NB] = gram
-
-    piece = 2 * NB // nz
-    mine = pl.ds(pl.multiple_of(z * piece, piece), piece)
-    copies = []
-    for o in range(1, nz):
-        theirs = pl.multiple_of(lax.rem(z + o, nz) * piece, piece)
-        copies.append(
-            pltpu.make_async_remote_copy(
-                src_ref=part.at[pl.ds(theirs, piece)],
-                dst_ref=zin.at[o - 1],
-                send_sem=zsend.at[o - 1],
-                recv_sem=zrecv.at[o - 1],
-                device_id=(cut, zpeers[o - 1]),
-                device_id_type=MESH,
-            )
-        )
-        copies[-1].start()
-    summed = part[mine]
-    for o in range(1, nz):
-        copies[o - 1].wait()
-        summed = summed + zin[o - 1]
-    mid[...] = summed
-    copies = []
-    for o in range(1, nx):
-        copies.append(
-            pltpu.make_async_remote_copy(
-                src_ref=mid,
-                dst_ref=xin.at[o - 1],
-                send_sem=xsend.at[o - 1],
-                recv_sem=xrecv.at[o - 1],
-                device_id=(cut, xpeers[o - 1]),
-                device_id_type=MESH,
-            )
-        )
-        copies[-1].start()
-    for o in range(1, nx):
-        copies[o - 1].wait()
-        summed = summed + xin[o - 1]
-    full[mine] = summed
-    copies = []
-    for o in range(1, nz):
-        copies.append(
-            pltpu.make_async_remote_copy(
-                src_ref=full.at[mine],
-                dst_ref=full.at[mine],
-                send_sem=gsend.at[o - 1],
-                recv_sem=grecv.at[o - 1],
-                device_id=(cut, zpeers[o - 1]),
-                device_id_type=MESH,
-            )
-        )
-        copies[-1].start()
-    for copy in copies:
-        copy.wait()
+    cpart[...] = cross
+    cross_z = share(cpart, czin, czsend, czrecv, zpeers)
+    gmid[...] = collect(gram_z, tight, gzin)
+    gram_x = share(gmid, gxin, gxsend, gxrecv, xpeers)
+    cmid[...] = collect(cross_z, cross, czin)
+    cross_x = share(cmid, cxin, cxsend, cxrecv, xpeers)
+    tight = collect(gram_x, gmid[...], gxin)
 
     across = lax.broadcasted_iota(jnp.int32, (NB, BS), 1)
     down = lax.broadcasted_iota(jnp.int32, (NB, BS), 0)
-    right = full[0:NB]
-    left = full[NB : 2 * NB] + jnp.where(across == down, 1.0, 0.0)
+    loose = [tight if g == 0 else pltpu.roll(tight, BS - NB * g, 1) for g in range(W)]
+    whole = jnp.where(across < NB, jnp.concatenate(loose, axis=0), 0.0)
+    whole = whole + jnp.where((across == down) | (across == down + NB), 1.0, 0.0)
     for j in range(NB):
-        column = left[:, j : j + 1]
-        pivot = 1.0 / left[j : j + 1, j : j + 1]
-        lrow = left[j : j + 1] * pivot
-        rrow = right[j : j + 1] * pivot
-        left = jnp.where(down == j, lrow, left - column * lrow)
-        right = jnp.where(down == j, rrow, right - column * rrow)
+        row_j = whole[j : j + 1] * (1.0 / whole[j : j + 1, j : j + 1])
+        whole = jnp.where(down == j, row_j, whole - whole[:, j : j + 1] * row_j)
+    summed = collect(cross_x, cmid[...], cxin)
+    tall = jnp.concatenate(
+        [jnp.zeros((NB, BS), F32), summed, jnp.zeros((2 * NB, BS), F32)], axis=0
+    )
+    right = jnp.dot(whole, tall, preferred_element_type=F32, precision=lax.Precision.HIGHEST)
     solved = right.astype(BF16).astype(F32)
     for g in range(W):
         above_rows = [jnp.zeros((NB, BS), F32)] * g
@@ -350,17 +369,20 @@
 
 def body(nz, nx, ncut, vectors, blocks, block_cols, counts, lower_end, upper_end, coeffs):
     blocks = blocks.reshape(RB * MAXB, BS, BS)
-    hbm = pl.BlockSpec(memory_space=pl.ANY)
-    smem = pl.BlockSpec(memory_space=pltpu.SMEM)
+    hbm = pl.BlockSpec(memory_space=pltpu.HBM)
     stage = pltpu.VMEM((W * MAXB + 1, BS, BS), BF16)
     dma = pltpu.SemaphoreType.DMA
-    piece = 2 * NB // nz
     return pl.pallas_call(
         functools.partial(kernel, nz, nx, ncut),
         out_shape=jax.ShapeDtypeStruct((OWN, BS), BF16),
-        in_specs=[hbm, hbm, smem, smem, smem, smem, smem],
+        in_specs=[hbm] * 7,
         out_specs=pl.BlockSpec(memory_space=pltpu.VMEM),
         scratch_shapes=[
+            pltpu.SMEM((MAXB, RB), jnp.int32),
+            pltpu.SMEM((RB,), jnp.int32),
+            pltpu.SMEM((1,), F32),
+            pltpu.SMEM((1,), F32),
+            pltpu.SMEM((1, DEG + 1), F32),
             stage,
             stage,
             stage,
@@ -373,22 +395,21 @@
             pltpu.VMEM((HALO, BS), BF16),
             pltpu.VMEM((HALO, BS), BF16),
             pltpu.VMEM((2, HALO, BS), F32),
-            pltpu.VMEM((2 * NB, BS), F32),
-            pltpu.VMEM((nz - 1, piece, BS), F32),
-            pltpu.VMEM((nx - 1, piece, BS), F32),
-            pltpu.VMEM((piece, BS), F32),
-            pltpu.VMEM((2 * NB, BS), F32),
+            pltpu.VMEM((8, BS), F32),
+            pltpu.VMEM((nz - 1, 8, BS), F32),
+            pltpu.VMEM((8, BS), F32),
+            pltpu.VMEM((nx - 1, 8, BS), F32),
+            pltpu.VMEM((NB, BS), F32),
+            pltpu.VMEM((nz - 1, NB, BS), F32),
+            pltpu.VMEM((NB, BS), F32),
+            pltpu.VMEM((nx - 1, NB, BS), F32),
+            dma((5,)),
             dma((QUADS,)),
             dma,
-            dma((2, 2)),
-            dma((2, 2)),
+            dma((2, 2, 2)),
+            dma((2, 2, 2)),
             dma((2,)),
-            dma((nz - 1,)),
-            dma((nz - 1,)),
-            dma((nx - 1,)),
-            dma((nx - 1,)),
-            dma((nz - 1,)),
-            dma((nz - 1,)),
+            *[dma((n,)) for n in 2 * [nz - 1, nz - 1, nx - 1, nx - 1]],
         ],
         compiler_params=pltpu.CompilerParams(
             collective_id=0, has_side_effects=True, vmem_limit_bytes=60 * 1024 * 1024

time: 108 us -> 95.2 us (0.88)
  Pallas kernels: 104 us -> 91.8 us
    pallas_call x1, Pallas kernels: 104 us -> 91.8 us  [body(): pl.pallas_call(functools.partial(kernel, nz, nx, ncut), out_shape=jax.Sha...]
where the time goes in v2:
time: 95.2 us; the launch traced here: 95 us
  Pallas kernels  91.8 us (96%)
  local copies, waits for them, and re-layouts  1.87 us (2%)
  between operations  1.3 us (1%)
    pallas_call x1, Pallas kernels, body(): pl.pallas_call(functools.partial(kernel, nz, nx, ncut), out_shape=jax.Sha...  91.8 us

profile of v2, /device:TPU:8, one launch (start us, length us, event | category | flops | bytes accessed | tf_op | source)
XLA Modules:
  0.0 95.0 jit_solution(18053669341888125643)
XLA Ops:
  1.3 91.8 %shard_map.73 = bf16[2048,128]{1,0:T(8,128)(2,1)} custom-call(bf16[2048,128]{1,0:T(8,128)(2,1)} %vec.1, bf16[128,128,128]{2,1,0:T(8,128)(2,1)} %bitcast.2, s32[8,16]{1,0:T(8,128)} %bitcast.3, s32[16]{0:T(128)} %counts_in.1, f32[1]{0:T(128)S(6)} %copy.9.lower_in, f32[1]{0:T(128)S(6)} %copy.10.upper_in, f32[1,7]{1,0:T(1,128)} %coeffs_in.1), custom_call_target="tpu_custom_call" | custom-call | tf_op jit(solution)/shard_map/pallas_call | solution.py:375
  93.1 1.9 %copy.11 = bf16[2048,128]{1,0:T(8,128)(2,1)} copy(bf16[2048,128]{1,0:T(8,128)(2,1)} %shard_map.73) | data formatting | bytes 1048576

commit v3 on v2

--- a/solution.py
+++ b/solution.py
@@ -15,7 +15,9 @@
 NB = 32
 RB = 16
 HALO = W * BS
-PIECE = HALO // 2
+NP = 4
+PIECE = HALO // NP
+ROUNDS = PASSES * DEG // 2
 OWN = RB * BS
 QUADS = RB // W
 WIDE = 3 * W * BS
@@ -61,6 +63,12 @@
     packed,
     arrived,
     acc,
+    halo,
+    ahead,
+    fetched,
+    known,
+    middle,
+    corner,
     gpart,
     gzin,
     gmid,
@@ -74,6 +82,9 @@
     vec_sem,
     send_sem,
     recv_sem,
+    asend,
+    arecv,
+    csem,
     edge_sem,
     gzsend,
     gzrecv,
@@ -135,38 +146,77 @@
 
     pl.semaphore_wait(barrier, greeted)
 
-    def to_low(src, slot, p):
+    def side_copy(src, dst, sent, got, device):
         return pltpu.make_async_remote_copy(
             src_ref=src,
-            dst_ref=vbuf.at[slot, pl.ds(HALO + OWN + p * PIECE, PIECE)],
-            send_sem=send_sem.at[0, slot, p],
-            recv_sem=recv_sem.at[1, slot, p],
-            device_id=(cut, low),
+            dst_ref=dst,
+            send_sem=sent,
+            recv_sem=got,
+            device_id=(cut, device),
             device_id_type=MESH,
         )
 
-    def to_high(src, slot, p):
-        return pltpu.make_async_remote_copy(
-            src_ref=src,
-            dst_ref=vbuf.at[slot, pl.ds(p * PIECE, PIECE)],
-            send_sem=send_sem.at[1, slot, p],
-            recv_sem=recv_sem.at[0, slot, p],
-            device_id=(cut, high),
-            device_id_type=MESH,
-        )
-
-    def low_edge(slot, p):
-        return to_low(vbuf.at[slot, pl.ds(HALO + p * PIECE, PIECE)], slot, p)
-
-    def high_edge(slot, p):
-        return to_high(vbuf.at[slot, pl.ds(OWN + p * PIECE, PIECE)], slot, p)
-
-    for p in (0, 1):
+    def to_low(src, turn, p):
+        return side_copy(
+            src,
+            halo.at[turn, 1, pl.ds(p * PIECE, PIECE)],
+            send_sem.at[0, turn, p],
+            recv_sem.at[1, turn, p],
+            low,
+        )
+
+    def to_high(src, turn, p):
+        return side_copy(
+            src,
+            halo.at[turn, 0, pl.ds(p * PIECE, PIECE)],
+            send_sem.at[1, turn, p],
+            recv_sem.at[0, turn, p],
+            high,
+        )
+
+    def low_edge(slot, turn, p):
+        return to_low(vbuf.at[slot, pl.ds(p * PIECE, PIECE)], turn, p)
+
+    def high_edge(slot, turn, p):
+        return to_high(vbuf.at[slot, pl.ds(OWN - HALO + p * PIECE, PIECE)], turn, p)
+
+    def low_ahead(turn, p):
+        at = pl.ds(p * PIECE, PIECE)
+        return side_copy(
+            ahead.at[0, at],
+            fetched.at[turn, 1, at],
+            asend.at[0, turn, p],
+            arecv.at[1, turn, p],
+            low,
+        )
+
+    def high_ahead(turn, p):
+        at = pl.ds(p * PIECE, PIECE)
+        return side_copy(
+            ahead.at[1, at],
+            fetched.at[turn, 0, at],
+            asend.at[1, turn, p],
+            arecv.at[0, turn, p],
+            high,
+        )
+
+    low_corner = side_copy(
+        dense.at[0, :, pl.ds(0, HALO)], corner.at[1], csem.at[0, 0], csem.at[1, 1], low
+    )
+    high_corner = side_copy(
+        dense.at[QUADS - 1, :, pl.ds(2 * HALO, HALO)],
+        corner.at[0],
+        csem.at[0, 1],
+        csem.at[1, 0],
+        high,
+    )
+
+    for p in range(NP):
         to_high(vec.at[pl.ds(OWN - HALO + p * PIECE, PIECE)], 0, p).start()
         to_low(vec.at[pl.ds(p * PIECE, PIECE)], 0, p).start()
 
     vec_copy.wait()
-    vbuf[0, pl.ds(HALO, OWN)] = start[...]
+    vbuf[0] = start[...]
     first = start[...].astype(F32)
     ybuf[0] = first
     ybuf[1] = jnp.zeros((OWN, BS), F32)
@@ -191,89 +241,165 @@
 
         lax.fori_loop(0, W, place, 0)
 
+    low_corner.start()
+    high_corner.start()
+
+    def factors(term):
+        opening = term == 0
+        scale = jnp.where(opening, 1.0, 2.0) * inverse
+        return scale, scale * centre, jnp.where(opening, 0.0, 1.0)
+
+    def recur(now, new, rows, product, scales):
+        scale, shift, keep = scales
+        return scale * product - shift * ybuf[now, rows] - keep * ybuf[new, rows]
+
+    def settle(new, rows, upcoming, term):
+        closing = term == DEG - 1
+        summed = total[rows] + coeffs[0, term + 1] * upcoming
+        value = jnp.where(closing, summed, upcoming)
+        total[rows] = jnp.where(closing, coeffs[0, 0] * summed, summed)
+        ybuf[new, rows] = value
+        vbuf[new, rows] = value.astype(BF16)
+
+    def inner(now, new, term, scales):
+        pair = 2 * BS
+        wide = (2 * W + 2) * BS
+        for q in (1, 2):
+            for j in (0, 1):
+                at = q * HALO + j * pair
+                product = dot(
+                    dense[q, j * pair : (j + 1) * pair, j * pair : j * pair + wide],
+                    vbuf[now, pl.ds(at - HALO, wide)],
+                )
+                rows = pl.ds(at, pair)
+                settle(new, rows, recur(now, new, rows, product, scales), term)
+
+    top, bottom = pl.ds(0, HALO), pl.ds(OWN - HALO, HALO)
+
+    def own_part(now, new, scales):
+        product = dot(dense[QUADS - 1, :, : 2 * HALO], vbuf[now, pl.ds(OWN - 2 * HALO, 2 * HALO)])
+        acc[1] = recur(now, new, bottom, product, scales)
+        product = dot(dense[0, :, HALO:], vbuf[now, pl.ds(0, 2 * HALO)])
+        acc[0] = recur(now, new, top, product, scales)
+
+    def bottom_piece(src, p, scales):
+        inside = slice(p * PIECE, (p + 1) * PIECE)
+        deep = (p + 1) * PIECE
+        product = dot(dense[QUADS - 1, inside, 2 * HALO : 2 * HALO + deep], src[pl.ds(0, deep)])
+        return acc[1, inside] + scales[0] * product
+
+    def top_piece(src, p, scales):
+        inside = slice(p * PIECE, (p + 1) * PIECE)
+        product = dot(
+            dense[0, inside, p * PIECE : HALO], src[pl.ds(p * PIECE, HALO - p * PIECE)]
+        )
+        return acc[0, inside] + scales[0] * product
+
+    def edges(new, turn):
+        return [f(new, turn, p) for f in (high_edge, low_edge) for p in range(NP)]
+
     def step(k, carry):
         now = lax.rem(k, 2)
         new = 1 - now
-        term = lax.rem(k, DEG)
-        opening = term == 0
-        closing = term == DEG - 1
-        scale = jnp.where(opening, 1.0, 2.0) * inverse
-        shift = scale * centre
-        keep = jnp.where(opening, 0.0, 1.0)
-        weight = coeffs[0, term + 1]
-        first_weight = coeffs[0, 0]
-
-        def finish(at, count, product):
-            rows = pl.ds(at, count)
-            upcoming = (
-                scale * product - shift * ybuf[now, rows] - keep * ybuf[new, rows]
-            )
-            summed = total[rows] + weight * upcoming
-            value = jnp.where(closing, summed, upcoming)
-            total[rows] = jnp.where(closing, first_weight * summed, summed)
-            ybuf[new, rows] = value
-            vbuf[new, pl.ds(HALO + at, count)] = value.astype(BF16)
-
-        half_rows = 2 * BS
-        wide = (2 * W + 2) * BS
-        def inner(n, carry):
-            q, j = 1 + lax.div(n, 2), lax.rem(n, 2)
-            at = pl.multiple_of(HALO + n * half_rows, half_rows)
-            within = pl.multiple_of(j * half_rows, half_rows)
-            product = dot(
-                dense[q, pl.ds(within, half_rows), pl.ds(within, wide)],
-                vbuf[now, pl.ds(at, wide)],
-            )
-            finish(at, half_rows, product)
-            return carry
-
-        lax.fori_loop(0, 4, inner, 0)
-        acc[0] = dot(dense[0, :, HALO:], vbuf[now, pl.ds(HALO, 2 * HALO)])
-        acc[1] = dot(dense[QUADS - 1, :, : 2 * HALO], vbuf[now, pl.ds(OWN - HALO, 2 * HALO)])
+        scales = factors(k)
+        own_part(now, new, scales)
+        inner(now, new, k, scales)
 
         @pl.when(k > 0)
         def _():
-            for p in (0, 1):
-                low_edge(new, p).wait_send()
-                high_edge(new, p).wait_send()
-
-        more = k < PASSES * DEG - 1
-        for p in (0, 1):
-            low_edge(now, p).wait_recv()
-            inside = slice(p * PIECE, (p + 1) * PIECE)
-            deep = (p + 1) * PIECE
-            finish(
-                OWN - HALO + p * PIECE,
-                PIECE,
-                acc[1, inside]
-                + dot(dense[QUADS - 1, inside, 2 * HALO : 2 * HALO + deep], vbuf[now, pl.ds(HALO + OWN, deep)]),
+            for copy in edges(new, new):
+                copy.wait_send()
+
+        for p in range(NP):
+            low_edge(now, now, p).wait_recv()
+            settle(
+                new,
+                pl.ds(OWN - HALO + p * PIECE, PIECE),
+                bottom_piece(halo.at[now, 1], p, scales),
+                k,
             )
+            high_edge(new, new, p).start()
+        for p in range(NP):
+            high_edge(now, now, p).wait_recv()
+        for p in range(NP):
+            settle(new, pl.ds(p * PIECE, PIECE), top_piece(halo.at[now, 0], p, scales), k)
+            low_edge(new, new, p).start()
+        return carry
+
+    lax.fori_loop(0, 2, step, 0)
+    low_corner.wait()
+    high_corner.wait()
+    for copy in edges(1, 1):
+        copy.wait_send()
+
+    def double(j, carry):
+        turn = lax.rem(j + 1, 2)
+        later = 1 - turn
+        term = lax.rem(2 * j, DEG)
+        scales = factors(term)
+
+        @pl.when(j > 1)
+        def _():
+            for p in range(NP):
+                low_ahead(later, p).wait_send()
+                high_ahead(later, p).wait_send()
+
+        own_part(0, 1, scales)
+        ahead[1] = acc[1].astype(BF16)
+        for p in range(NP):
+            high_ahead(turn, p).start()
+        ahead[0] = acc[0].astype(BF16)
+        for p in range(NP):
+            low_ahead(turn, p).start()
+        known[1] = scales[0] * dot(corner[1], vbuf[0, bottom])
+        known[0] = scales[0] * dot(corner[0], vbuf[0, top])
+        inner(0, 1, term, scales)
+        for p in range(NP):
+            low_edge(0, turn, p).wait_recv()
+        for p in range(NP):
+            rows = pl.ds(OWN - HALO + p * PIECE, PIECE)
+            settle(1, rows, bottom_piece(halo.at[turn, 1], p, scales), term)
+        for p in range(NP):
+            high_edge(0, turn, p).wait_recv()
+        for p in range(NP):
+            rows = pl.ds(p * PIECE, PIECE)
+            settle(1, rows, top_piece(halo.at[turn, 0], p, scales), term)
+
+        for copy in edges(0, turn):
+            copy.wait_send()
+        scales = factors(term + 1)
+        own_part(1, 0, scales)
+        inner(1, 0, term + 1, scales)
+        more = j < ROUNDS - 1
+        for p in range(NP):
+            low_ahead(turn, p).wait_recv()
+            at = pl.ds(p * PIECE, PIECE)
+            middle[1, at] = (fetched[turn, 1, at].astype(F32) + known[1, at]).astype(BF16)
+            rows = pl.ds(OWN - HALO + p * PIECE, PIECE)
+            settle(0, rows, bottom_piece(middle.at[1], p, scales), term + 1)
 
             @pl.when(more)
             def _(p=p):
-                high_edge(new, p).start()
-
-        for p in (0, 1):
-            high_edge(now, p).wait_recv()
-        for p in (0, 1):
-            inside = slice(p * PIECE, (p + 1) * PIECE)
-            finish(
-                p * PIECE,
-                PIECE,
-                acc[0, inside] + dot(dense[0, inside, p * PIECE : HALO], vbuf[now, pl.ds(p * PIECE, HALO - p * PIECE)]),
-            )
+                high_edge(0, later, p).start()
+
+        for p in range(NP):
+            high_ahead(turn, p).wait_recv()
+            at = pl.ds(p * PIECE, PIECE)
+            middle[0, at] = (fetched[turn, 0, at].astype(F32) + known[0, at]).astype(BF16)
+        for p in range(NP):
+            settle(0, pl.ds(p * PIECE, PIECE), top_piece(middle.at[0], p, scales), term + 1)
 
             @pl.when(more)
             def _(p=p):
-                low_edge(new, p).start()
+                low_edge(0, later, p).start()
 
         return carry
 
-    lax.fori_loop(0, PASSES * DEG, step, 0)
-    last = (PASSES * DEG) % 2
-    for p in (0, 1):
-        low_edge(1 - last, p).wait_send()
-        high_edge(1 - last, p).wait_send()
+    lax.fori_loop(1, ROUNDS, double, 0)
+    for p in range(NP):
+        low_ahead(ROUNDS % 2, p).wait_send()
+        high_ahead(ROUNDS % 2, p).wait_send()
+    last = 0
 
     lane = lax.broadcasted_iota(jnp.int32, (HALO, BS), 1)
     strip = jnp.zeros((HALO, BS), F32)
@@ -334,7 +460,7 @@
     gram_z = share(gpart, gzin, gzsend, gzrecv, zpeers)
     cross = jnp.zeros((NB, BS), F32)
     for g in range(W):
-        mine = vbuf[last, pl.ds(HALO + g * HALO, HALO)]
+        mine = vbuf[last, pl.ds(g * HALO, HALO)]
         cross = cross + tdot(boundary, mine)[g * NB : (g + 1) * NB]
     cpart[...] = cross
     cross_z = share(cpart, czin, czsend, czrecv, zpeers)
@@ -388,13 +514,19 @@
             stage,
             stage,
             pltpu.VMEM((QUADS, HALO, WIDE), BF16),
-            pltpu.VMEM((2, OWN + 2 * HALO, BS), BF16),
+            pltpu.VMEM((2, OWN, BS), BF16),
             pltpu.VMEM((2, OWN, BS), F32),
             pltpu.VMEM((OWN, BS), F32),
             pltpu.VMEM((OWN, BS), BF16),
             pltpu.VMEM((HALO, BS), BF16),
             pltpu.VMEM((HALO, BS), BF16),
             pltpu.VMEM((2, HALO, BS), F32),
+            pltpu.VMEM((2, 2, HALO, BS), BF16),
+            pltpu.VMEM((2, HALO, BS), BF16),
+            pltpu.VMEM((2, 2, HALO, BS), BF16),
+            pltpu.VMEM((2, HALO, BS), F32),
+            pltpu.VMEM((2, HALO, BS), BF16),
+            pltpu.VMEM((2, HALO, HALO), BF16),
             pltpu.VMEM((8, BS), F32),
             pltpu.VMEM((nz - 1, 8, BS), F32),
             pltpu.VMEM((8, BS), F32),
@@ -406,8 +538,8 @@
             dma((5,)),
             dma((QUADS,)),
             dma,
-            dma((2, 2, 2)),
-            dma((2, 2, 2)),
+            *[dma((2, 2, NP))] * 4,
+            dma((2, 2)),
             dma((2,)),
             *[dma((n,)) for n in 2 * [nz - 1, nz - 1, nx - 1, nx - 1]],
         ],

time: 95.2 us -> 88.9 us (0.934)
  Pallas kernels: 91.8 us -> 85.6 us
    pallas_call x1, Pallas kernels: 91.8 us -> 85.6 us  [body(): pl.pallas_call(functools.partial(kernel, nz, nx, ncut), out_shape=jax.Sha...]
where the time goes in v3:
time: 88.9 us; the launch traced here: 88.7 us
  Pallas kernels  85.6 us (96%)
  local copies, waits for them, and re-layouts  1.87 us (2%)
  between operations  1.3 us (1%)
    pallas_call x1, Pallas kernels, body(): pl.pallas_call(functools.partial(kernel, nz, nx, ncut), out_shape=jax.Sha...  85.6 us
    unnamed x1, local copies, waits for them, and re-layouts  1.87 us

profile of v3, /device:TPU:8, one launch (start us, length us, event | category | flops | bytes accessed | tf_op | source)
XLA Modules:
  0.0 88.7 jit_solution(3889050488365452441)
XLA Ops:
  1.3 85.6 %shard_map.73 = bf16[2048,128]{1,0:T(8,128)(2,1)} custom-call(bf16[2048,128]{1,0:T(8,128)(2,1)} %vec.1, bf16[128,128,128]{2,1,0:T(8,128)(2,1)} %bitcast.2, s32[8,16]{1,0:T(8,128)} %bitcast.3, s32[16]{0:T(128)} %counts_in.1, f32[1]{0:T(128)S(6)} %copy.9.lower_in, f32[1]{0:T(128)S(6)} %copy.10.upper_in, f32[1,7]{1,0:T(1,128)} %coeffs_in.1), custom_call_target="tpu_custom_call" | custom-call | tf_op jit(solution)/shard_map/pallas_call | solution.py:501
  86.9 1.9 %copy.11 = bf16[2048,128]{1,0:T(8,128)(2,1)} copy(bf16[2048,128]{1,0:T(8,128)(2,1)} %shard_map.73) | data formatting | bytes 1048576

commit v4 on v3

--- a/solution.py
+++ b/solution.py
@@ -15,7 +15,7 @@
 NB = 32
 RB = 16
 HALO = W * BS
-NP = 4
+NP = 2
 PIECE = HALO // NP
 ROUNDS = PASSES * DEG // 2
 OWN = RB * BS
@@ -67,6 +67,7 @@
     ahead,
     fetched,
     known,
+    early,
     middle,
     corner,
     gpart,
@@ -84,7 +85,10 @@
     recv_sem,
     asend,
     arecv,
-    csem,
+    csend,
+    crecv,
+    wsend,
+    wrecv,
     edge_sem,
     gzsend,
     gzrecv,
@@ -126,6 +130,7 @@
         copy.start()
         block_copies.append(copy)
 
+    corner[...] = jnp.zeros((2, HALO, HALO), BF16)
     barrier = pltpu.get_barrier_semaphore()
     greeted = 0
     for other in [low, high, *zpeers, *xpeers]:
@@ -200,16 +205,35 @@
             high,
         )
 
-    low_corner = side_copy(
-        dense.at[0, :, pl.ds(0, HALO)], corner.at[1], csem.at[0, 0], csem.at[1, 1], low
-    )
-    high_corner = side_copy(
-        dense.at[QUADS - 1, :, pl.ds(2 * HALO, HALO)],
-        corner.at[0],
-        csem.at[0, 1],
-        csem.at[1, 0],
-        high,
-    )
+    def low_corner(i):
+        at, lanes = pl.ds(i * BS, BS), pl.ds(i * BS, (W - i) * BS)
+        return side_copy(
+            dense.at[0, at, lanes], corner.at[1, at, lanes], csend.at[0, i], crecv.at[1, i], low
+        )
+
+    def high_corner(i):
+        at, lanes = pl.ds(i * BS, BS), pl.ds(0, (i + 1) * BS)
+        return side_copy(
+            dense.at[QUADS - 1, at, pl.ds(2 * HALO, (i + 1) * BS)],
+            corner.at[0, at, lanes],
+            csend.at[1, i],
+            crecv.at[0, i],
+            high,
+        )
+
+    def swapped(side, i):
+        at = pl.ds(i * BS, BS)
+        lanes = pl.ds(i * BS, (W - i) * BS) if side else pl.ds(0, (i + 1) * BS)
+        return pltpu.make_async_remote_copy(
+            src_ref=corner.at[side, at, lanes],
+            dst_ref=corner.at[side, at, lanes],
+            send_sem=wsend.at[side, i],
+            recv_sem=wrecv.at[side, i],
+            device_id=(cut + 1 - 2 * lax.rem(cut, 2), row),
+            device_id_type=MESH,
+        )
+
+    halves = ((0, (0, W - 1)), (1, (1, W - 2)))
 
     for p in range(NP):
         to_high(vec.at[pl.ds(OWN - HALO + p * PIECE, PIECE)], 0, p).start()
@@ -241,9 +265,6 @@
 
         lax.fori_loop(0, W, place, 0)
 
-    low_corner.start()
-    high_corner.start()
-
     def factors(term):
         opening = term == 0
         scale = jnp.where(opening, 1.0, 2.0) * inverse
@@ -326,9 +347,26 @@
             low_edge(new, new, p).start()
         return carry
 
-    lax.fori_loop(0, 2, step, 0)
-    low_corner.wait()
-    high_corner.wait()
+    lax.fori_loop(0, 1, step, 0)
+    for parity, mine in halves:
+
+        @pl.when(lax.rem(cut, 2) == parity)
+        def _(mine=mine):
+            for i in mine:
+                high_corner(i).start()
+                low_corner(i).start()
+
+    lax.fori_loop(1, 2, step, 0)
+    for parity, mine in halves:
+
+        @pl.when(lax.rem(cut, 2) == parity)
+        def _(mine=mine):
+            for i in mine:
+                for copy in (high_corner(i), low_corner(i)):
+                    copy.wait()
+                for side in (0, 1):
+                    swapped(side, i).start()
+
     for copy in edges(1, 1):
         copy.wait_send()
 
@@ -351,26 +389,46 @@
         ahead[0] = acc[0].astype(BF16)
         for p in range(NP):
             low_ahead(turn, p).start()
+        inner(0, 1, term, scales)
+        early[1] = dot(dense[QUADS - 1, :, :HALO], vbuf[1, pl.ds(OWN - 2 * HALO, HALO)])
+        early[0] = dot(dense[0, :, 2 * HALO :], vbuf[1, pl.ds(HALO, HALO)])
+
+        @pl.when(j == 1)
+        def _():
+            for parity, mine in halves:
+                other = halves[1 - parity][1]
+
+                @pl.when(lax.rem(cut, 2) == parity)
+                def _(mine=mine, other=other):
+                    for side in (0, 1):
+                        for i in mine:
+                            swapped(side, i).wait_send()
+                        for i in other:
+                            swapped(side, i).wait_recv()
+
         known[1] = scales[0] * dot(corner[1], vbuf[0, bottom])
         known[0] = scales[0] * dot(corner[0], vbuf[0, top])
-        inner(0, 1, term, scales)
         for p in range(NP):
             low_edge(0, turn, p).wait_recv()
-        for p in range(NP):
-            rows = pl.ds(OWN - HALO + p * PIECE, PIECE)
-            settle(1, rows, bottom_piece(halo.at[turn, 1], p, scales), term)
+        product = dot(dense[QUADS - 1, :, 2 * HALO :], halo[turn, 1])
+        settle(1, bottom, acc[1] + scales[0] * product, term)
+        scales = factors(term + 1)
+        product = early[1] + dot(dense[QUADS - 1, :, HALO : 2 * HALO], vbuf[1, bottom])
+        acc[1] = recur(1, 0, bottom, product, scales)
         for p in range(NP):
             high_edge(0, turn, p).wait_recv()
-        for p in range(NP):
-            rows = pl.ds(p * PIECE, PIECE)
-            settle(1, rows, top_piece(halo.at[turn, 0], p, scales), term)
-
+        product = dot(dense[0, :, :HALO], halo[turn, 0])
+        settle(1, top, acc[0] + factors(term)[0] * product, term)
+        product = early[0] + dot(dense[0, :, HALO : 2 * HALO], vbuf[1, top])
+        acc[0] = recur(1, 0, top, product, scales)
         for copy in edges(0, turn):
             copy.wait_send()
-        scales = factors(term + 1)
-        own_part(1, 0, scales)
-        inner(1, 0, term + 1, scales)
         more = j < ROUNDS - 1
+
+        @pl.when(jnp.logical_not(more))
+        def _():
+            inner(1, 0, term + 1, scales)
+
         for p in range(NP):
             low_ahead(turn, p).wait_recv()
             at = pl.ds(p * PIECE, PIECE)
@@ -392,6 +450,10 @@
             @pl.when(more)
             def _(p=p):
                 low_edge(0, later, p).start()
+
+        @pl.when(more)
+        def _():
+            inner(1, 0, term + 1, scales)
 
         return carry
 
@@ -525,6 +587,7 @@
             pltpu.VMEM((2, HALO, BS), BF16),
             pltpu.VMEM((2, 2, HALO, BS), BF16),
             pltpu.VMEM((2, HALO, BS), F32),
+            pltpu.VMEM((2, HALO, BS), F32),
             pltpu.VMEM((2, HALO, BS), BF16),
             pltpu.VMEM((2, HALO, HALO), BF16),
             pltpu.VMEM((8, BS), F32),
@@ -539,7 +602,7 @@
             dma((QUADS,)),
             dma,
             *[dma((2, 2, NP))] * 4,
-            dma((2, 2)),
+            *[dma((2, W))] * 4,
             dma((2,)),
             *[dma((n,)) for n in 2 * [nz - 1, nz - 1, nx - 1, nx - 1]],
         ],

time: 88.9 us -> 81.8 us (0.920)
  Pallas kernels: 85.6 us -> 78.5 us
    pallas_call x1, Pallas kernels: 85.6 us -> 78.5 us  [body(): pl.pallas_call(functools.partial(kernel, nz, nx, ncut), out_shape=jax.Sha...]
where the time goes in v4:
time: 81.8 us; the launch traced here: 81.7 us
  Pallas kernels  78.5 us (96%)
  local copies, waits for them, and re-layouts  1.87 us (2%)
  between operations  1.3 us (2%)
    pallas_call x1, Pallas kernels, body(): pl.pallas_call(functools.partial(kernel, nz, nx, ncut), out_shape=jax.Sha...  78.5 us
    unnamed x1, local copies, waits for them, and re-layouts  1.87 us

profile of v4, /device:TPU:8, one launch (start us, length us, event | category | flops | bytes accessed | tf_op | source)
XLA Modules:
  0.0 81.7 jit_solution(10983087145751216751)
XLA Ops:
  1.3 78.5 %shard_map.73 = bf16[2048,128]{1,0:T(8,128)(2,1)} custom-call(bf16[2048,128]{1,0:T(8,128)(2,1)} %vec.1, bf16[128,128,128]{2,1,0:T(8,128)(2,1)} %bitcast.2, s32[8,16]{1,0:T(8,128)} %bitcast.3, s32[16]{0:T(128)} %counts_in.1, f32[1]{0:T(128)S(6)} %copy.9.lower_in, f32[1]{0:T(128)S(6)} %copy.10.upper_in, f32[1,7]{1,0:T(1,128)} %coeffs_in.1), custom_call_target="tpu_custom_call" | custom-call | tf_op jit(solution)/shard_map/pallas_call | solution.py:563
  79.8 1.9 %copy.11 = bf16[2048,128]{1,0:T(8,128)(2,1)} copy(bf16[2048,128]{1,0:T(8,128)(2,1)} %shard_map.73) | data formatting | bytes 1048576

commit v5 on v4

--- a/solution.py
+++ b/solution.py
@@ -425,10 +425,7 @@
             copy.wait_send()
         more = j < ROUNDS - 1
 
-        @pl.when(jnp.logical_not(more))
-        def _():
-            inner(1, 0, term + 1, scales)
-
+        inner(1, 0, term + 1, scales)
         for p in range(NP):
             low_ahead(turn, p).wait_recv()
             at = pl.ds(p * PIECE, PIECE)
@@ -450,10 +447,6 @@
             @pl.when(more)
             def _(p=p):
                 low_edge(0, later, p).start()
-
-        @pl.when(more)
-        def _():
-            inner(1, 0, term + 1, scales)
 
         return carry
 
@@ -562,7 +555,7 @@
     dma = pltpu.SemaphoreType.DMA
     return pl.pallas_call(
         functools.partial(kernel, nz, nx, ncut),
-        out_shape=jax.ShapeDtypeStruct((OWN, BS), BF16),
+        out_shape=pltpu.VMEM((OWN, BS), BF16),
         in_specs=[hbm] * 7,
         out_specs=pl.BlockSpec(memory_space=pltpu.VMEM),
         scratch_shapes=[
@@ -607,7 +600,7 @@
             *[dma((n,)) for n in 2 * [nz - 1, nz - 1, nx - 1, nx - 1]],
         ],
         compiler_params=pltpu.CompilerParams(
-            collective_id=0, has_side_effects=True, vmem_limit_bytes=60 * 1024 * 1024
+            collective_id=0, has_side_effects=True, vmem_limit_bytes=59 * 1024 * 1024
         ),
     )(vectors, blocks, block_cols.T, counts, lower_end, upper_end, coeffs)
 

time: 81.8 us -> 78.9 us (0.965)
  Pallas kernels: 78.5 us -> 76.7 us
  local copies, waits for them, and re-layouts: 1.87 us -> 0.8 us
    pallas_call x1, Pallas kernels: 78.5 us -> 76.7 us  [body(): pl.pallas_call(functools.partial(kernel, nz, nx, ncut), out_shape=pltpu.V...]
    unnamed x1, local copies, waits for them, and re-layouts: 1.87 us -> 0.8 us
where the time goes in v5:
time: 78.9 us; the launch traced here: 78.8 us
  Pallas kernels  76.7 us (97%)
  between operations  1.3 us (2%)
  local copies, waits for them, and re-layouts  0.8 us (1%)
    pallas_call x1, Pallas kernels, body(): pl.pallas_call(functools.partial(kernel, nz, nx, ncut), out_shape=pltpu.V...  76.7 us

profile of v5, /device:TPU:8, one launch (start us, length us, event | category | flops | bytes accessed | tf_op | source)
XLA Modules:
  0.0 78.8 jit_solution(2033468283739007579)
XLA Ops:
  1.3 76.7 %shard_map.73 = bf16[2048,128]{1,0:T(8,128)(2,1)S(1)} custom-call(bf16[2048,128]{1,0:T(8,128)(2,1)} %vec.1, bf16[128,128,128]{2,1,0:T(8,128)(2,1)} %bitcast.2, s32[8,16]{1,0:T(8,128)} %bitcast.3, s32[16]{0:T(128)} %counts_in.1, f32[1]{0:T(128)S(6)} %copy.10.lower_in, f32[1]{0:T(128)S(6)} %copy.11.upper_in, f32[1,7]{1,0:T(1,128)} %coeffs_in.1), custom_call_target="tpu_custom_call" | custom-call | tf_op jit(solution)/shard_map/pallas_call | solution.py:556
  78.0 0.8 %copy.9 = bf16[2048,128]{1,0:T(8,128)(2,1)} copy(bf16[2048,128]{1,0:T(8,128)(2,1)S(1)} %shard_map.73) | data formatting | bytes 1048576

commit v6 on v5

--- a/solution.py
+++ b/solution.py
@@ -370,6 +370,32 @@
     for copy in edges(1, 1):
         copy.wait_send()
 
+    low_half = HALO // 2
+    groups = (
+        tuple(HALO + g * low_half for g in range(W)),
+        (0, low_half, OWN - HALO, OWN - low_half),
+    )
+    lane = lax.broadcasted_iota(jnp.int32, (low_half, BS), 1)
+
+    def boundary_half(h):
+        at = pl.ds(h * low_half, low_half)
+        return pltpu.make_async_remote_copy(
+            src_ref=packed.at[at],
+            dst_ref=arrived.at[at],
+            send_sem=edge_sem.at[0, h],
+            recv_sem=edge_sem.at[1, h],
+            device_id=(after, row),
+            device_id_type=MESH,
+        )
+
+    def send_boundary(h):
+        strip = jnp.zeros((low_half, BS), F32)
+        for g, first_row in enumerate(groups[h]):
+            turned = pltpu.roll(ybuf[0, pl.ds(first_row, low_half)], (NB * (g + 1)) % BS, 1)
+            strip = jnp.where(lane // NB == g, turned, strip)
+        packed[pl.ds(h * low_half, low_half)] = strip.astype(BF16)
+        boundary_half(h).start()
+
     def double(j, carry):
         turn = lax.rem(j + 1, 2)
         later = 1 - turn
@@ -426,6 +452,11 @@
         more = j < ROUNDS - 1
 
         inner(1, 0, term + 1, scales)
+
+        @pl.when(jnp.logical_not(more))
+        def _():
+            send_boundary(0)
+
         for p in range(NP):
             low_ahead(turn, p).wait_recv()
             at = pl.ds(p * PIECE, PIECE)
@@ -456,25 +487,22 @@
         high_ahead(ROUNDS % 2, p).wait_send()
     last = 0
 
-    lane = lax.broadcasted_iota(jnp.int32, (HALO, BS), 1)
-    strip = jnp.zeros((HALO, BS), F32)
-    for g in range(W):
-        turned = pltpu.roll(ybuf[last, g * HALO : (g + 1) * HALO], (NB * (g + 1)) % BS, 1)
-        strip = jnp.where(lane // NB == g, turned, strip)
-    packed[...] = strip.astype(BF16)
-    edge = pltpu.make_async_remote_copy(
-        src_ref=packed,
-        dst_ref=arrived,
-        send_sem=edge_sem.at[0],
-        recv_sem=edge_sem.at[1],
-        device_id=(after, row),
-        device_id_type=MESH,
-    )
-    edge.start()
-    edge.wait()
-    @pl.when(cut == 0)
-    def _():
-        arrived[...] = jnp.zeros((HALO, BS), BF16)
+    send_boundary(1)
+    square = jnp.zeros((BS, BS), F32)
+    cross = jnp.zeros((NB, BS), F32)
+    for h in (0, 1):
+        boundary_half(h).wait()
+        at = pl.ds(h * low_half, low_half)
+
+        @pl.when(cut == 0)
+        def _(at=at):
+            arrived[at] = jnp.zeros((low_half, BS), BF16)
+
+        boundary = arrived[at]
+        square = square + tdot(boundary, boundary)
+        for g, first_row in enumerate(groups[h]):
+            mine = vbuf[last, pl.ds(first_row, low_half)]
+            cross = cross + tdot(boundary, mine)[g * NB : (g + 1) * NB]
 
     def share(src, slots, sent, got, peers):
         copies = []
@@ -499,8 +527,6 @@
             summed = summed + slots[o]
         return summed
 
-    boundary = arrived[...]
-    square = tdot(boundary, boundary)
     eight = BS // W // W
     group = lax.broadcasted_iota(jnp.int32, (eight, BS), 1) // NB
     gram = jnp.zeros((NB, BS), F32)
@@ -513,10 +539,6 @@
         tight = jnp.where(group == g, pltpu.roll(rows, NB * g, 1) if g else rows, tight)
     gpart[...] = tight
     gram_z = share(gpart, gzin, gzsend, gzrecv, zpeers)
-    cross = jnp.zeros((NB, BS), F32)
-    for g in range(W):
-        mine = vbuf[last, pl.ds(g * HALO, HALO)]
-        cross = cross + tdot(boundary, mine)[g * NB : (g + 1) * NB]
     cpart[...] = cross
     cross_z = share(cpart, czin, czsend, czrecv, zpeers)
     gmid[...] = collect(gram_z, tight, gzin)
@@ -543,9 +565,10 @@
         above_rows = [jnp.zeros((NB, BS), F32)] * g
         below_rows = [jnp.zeros((NB, BS), F32)] * (W - 1 - g)
         spread = jnp.concatenate([*above_rows, solved, *below_rows], axis=0).astype(BF16)
-        correction = dot(boundary, spread)
-        rows = pl.ds(g * HALO, HALO)
-        out[rows] = (ybuf[last, rows] - correction).astype(BF16)
+        for h in (0, 1):
+            correction = dot(arrived[pl.ds(h * low_half, low_half)], spread)
+            rows = pl.ds(groups[h][g], low_half)
+            out[rows] = (ybuf[last, rows] - correction).astype(BF16)
 
 
 def body(nz, nx, ncut, vectors, blocks, block_cols, counts, lower_end, upper_end, coeffs):
@@ -596,7 +619,7 @@
             dma,
             *[dma((2, 2, NP))] * 4,
             *[dma((2, W))] * 4,
-            dma((2,)),
+            dma((2, 2)),
             *[dma((n,)) for n in 2 * [nz - 1, nz - 1, nx - 1, nx - 1]],
         ],
         compiler_params=pltpu.CompilerParams(

time: 78.9 us -> 79 us (level)
  no operation moved by 1% of the time
where the time goes in v6:
time: 79 us; the launch traced here: 78.9 us
  Pallas kernels  76.8 us (97%)
  between operations  1.3 us (2%)
  local copies, waits for them, and re-layouts  0.8 us (1%)
    pallas_call x1, Pallas kernels, body(): pl.pallas_call(functools.partial(kernel, nz, nx, ncut), out_shape=pltpu.V...  76.8 us

profile of v6, /device:TPU:8, one launch (start us, length us, event | category | flops | bytes accessed | tf_op | source)
XLA Modules:
  0.0 78.9 jit_solution(141271949778655133)
XLA Ops:
  1.3 76.8 %shard_map.73 = bf16[2048,128]{1,0:T(8,128)(2,1)S(1)} custom-call(bf16[2048,128]{1,0:T(8,128)(2,1)} %vec.1, bf16[128,128,128]{2,1,0:T(8,128)(2,1)} %bitcast.2, s32[8,16]{1,0:T(8,128)} %bitcast.3, s32[16]{0:T(128)} %counts_in.1, f32[1]{0:T(128)S(6)} %copy.10.lower_in, f32[1]{0:T(128)S(6)} %copy.11.upper_in, f32[1,7]{1,0:T(1,128)} %coeffs_in.1), custom_call_target="tpu_custom_call" | custom-call | tf_op jit(solution)/shard_map/pallas_call | solution.py:579
  78.1 0.8 %copy.9 = bf16[2048,128]{1,0:T(8,128)(2,1)} copy(bf16[2048,128]{1,0:T(8,128)(2,1)S(1)} %shard_map.73) | data formatting | bytes 1048576

commit v7 on v6

--- a/solution.py
+++ b/solution.py
@@ -283,16 +283,15 @@
         vbuf[new, rows] = value.astype(BF16)
 
     def inner(now, new, term, scales):
-        pair = 2 * BS
-        wide = (2 * W + 2) * BS
+        wide = (2 * W + 1) * BS
         for q in (1, 2):
-            for j in (0, 1):
-                at = q * HALO + j * pair
+            for i in range(W):
+                at = q * HALO + i * BS
                 product = dot(
-                    dense[q, j * pair : (j + 1) * pair, j * pair : j * pair + wide],
+                    dense[q, i * BS : (i + 1) * BS, i * BS : i * BS + wide],
                     vbuf[now, pl.ds(at - HALO, wide)],
                 )
-                rows = pl.ds(at, pair)
+                rows = pl.ds(at, BS)
                 settle(new, rows, recur(now, new, rows, product, scales), term)
 
     top, bottom = pl.ds(0, HALO), pl.ds(OWN - HALO, HALO)

time: 79 us -> 78.8 us (level)
  no operation moved by 1% of the time
where the time goes in v7:
time: 78.8 us; the launch traced here: 78.7 us
  Pallas kernels  76.6 us (97%)
  between operations  1.3 us (2%)
  local copies, waits for them, and re-layouts  0.8 us (1%)
    pallas_call x1, Pallas kernels, body(): pl.pallas_call(functools.partial(kernel, nz, nx, ncut), out_shape=pltpu.V...  76.6 us

profile of v7, /device:TPU:8, one launch (start us, length us, event | category | flops | bytes accessed | tf_op | source)
XLA Modules:
  0.0 78.7 jit_solution(1826029640682775477)
XLA Ops:
  1.3 76.6 %shard_map.73 = bf16[2048,128]{1,0:T(8,128)(2,1)S(1)} custom-call(bf16[2048,128]{1,0:T(8,128)(2,1)} %vec.1, bf16[128,128,128]{2,1,0:T(8,128)(2,1)} %bitcast.2, s32[8,16]{1,0:T(8,128)} %bitcast.3, s32[16]{0:T(128)} %counts_in.1, f32[1]{0:T(128)S(6)} %copy.10.lower_in, f32[1]{0:T(128)S(6)} %copy.11.upper_in, f32[1,7]{1,0:T(1,128)} %coeffs_in.1), custom_call_target="tpu_custom_call" | custom-call | tf_op jit(solution)/shard_map/pallas_call | solution.py:578
  77.9 0.8 %copy.9 = bf16[2048,128]{1,0:T(8,128)(2,1)} copy(bf16[2048,128]{1,0:T(8,128)(2,1)S(1)} %shard_map.73) | data formatting | bytes 1048576
